TPU v7x, 512 devices: a whole 4x8x8 slice. The times are simulated.
512 devices in a mesh: leaf: 32 (over y, x), near: 16 (over z, core).
Axes of the slice: x: 4, y: 8, z: 8, core: 2. Of those that a mesh axis runs over, the one named last changes fastest.
Arguments:
- input_point_values: bfloat16 [2048, 32, 256], P(('leaf', 'near')), may hold values from -6 to 6
- leaf_cluster_basis: bfloat16 [2048, 64, 256], P(('leaf', 'near')), may hold values from -0.375 to 0.375
- near_blocks: bfloat16 [2048, 7, 256, 256], P(('leaf', 'near')), may hold values from -0.125 to 0.125
- near_cols: int32 [2048, 7], P(('leaf', 'near')), may hold values from 0 to 2047, as said below
- leaf_transfer: bfloat16 [2048, 64, 64], P(('leaf', 'near')), may hold values from -0.375 to 0.375
- leaf_coupling: bfloat16 [8, 64, 64], replicated, may hold values from -0.3125 to 0.3125
- node_coupling: bfloat16 [512, 4, 64, 64], P(('leaf', 'near')), may hold values from -0.4375 to 0.4375
- level_transfer: bfloat16 [3, 2, 64, 64], replicated, may hold values from -0.5 to 0.5
- level_coupling: bfloat16 [3, 4, 64, 64], replicated, may hold values from -0.4375 to 0.4375
Outputs:
- product: float32 [2048, 32, 256], P(('leaf', 'near'))
Inputs may be any that keep to these rules, and one draw needn't show every extreme that they name: `near_cols`: row i lists each leaf j with (j - i) mod 2048 or (i - j) mod 2048 at most 3 exactly once; the first is i itself.
All inputs are finite; a program needn't handle non-finite values.
Results may differ from a plain program's by a relative error of at most 0.0003.
Values may be sent and summed in bfloat16 or wider, within the bound.
No kernel may reach another device: no remote copies, remote signals or barrier semaphores. Data moves between devices by JAX's collectives and lax.ppermute only.
A program may use at most 64 MiB of HBM per device.

v0:
```python
import jax
import jax.numpy as jnp
from jax import lax
from jax.sharding import PartitionSpec as P

NREACH = 3
COARSE = 3


OFFSETS = (-3, -2, 2, 3)
topmost_level = lax.Precision.HIGHEST


def with_halo(cells, sides, width):
    for axis, dim in sides:
        count = lax.axis_size(axis)
        head = lax.slice_in_dim(cells, 0, width, axis=dim)
        tail = lax.slice_in_dim(cells, cells.shape[dim] - width, cells.shape[dim], axis=dim)
        cells = jnp.concatenate(
            [
                lax.ppermute(tail, axis, [(i, (i + 1) % count) for i in range(count)]),
                cells,
                lax.ppermute(head, axis, [((i + 1) % count, i) for i in range(count)]),
            ],
            axis=dim,
        )
    return cells


def swapped(value, axis, stride):
    mask = 2**stride
    pairs = [(source, source ^ mask) for source in range(lax.axis_size(axis))]
    return lax.ppermute(value, axis, pairs)


def shifted(value, axis, steps):
    count = lax.axis_size(axis)
    pairs = [(source, (source + steps) % count) for source in range(count)]
    return lax.ppermute(value, axis, pairs)


def slot_weight(parity, position_index):
    if position_index == 0:
        return (parity == 1).astype(jnp.float32)
    if position_index == 3:
        return (parity == 0).astype(jnp.float32)
    return jnp.float32(1.0)


def local(
    input_point_values,
    leaf_cluster_basis,
    near_blocks,
    near_cols,
    leaf_transfer,
    leaf_coupling,
    node_coupling,
    level_transfer,
    level_coupling,
):
    position = lax.axis_index(("leaf", "near"))
    members = lax.axis_size(("leaf", "near"))
    leaf_dev = input_point_values.shape[0]
    window = with_halo(input_point_values, ((("leaf", "near"), 0),), NREACH)
    relative = jnp.mod(near_cols - position * leaf_dev + NREACH, leaf_dev * members)
    picked = jnp.take(window, relative, axis=0)
    near_sum = jnp.einsum("lkpq,lksq->lsp", near_blocks, picked, preferred_element_type=jnp.float32)
    leaf_multipoles = jnp.einsum(
        "zcw,znw->zcn", input_point_values, leaf_cluster_basis, preferred_element_type=jnp.float32
    )
    rim_moments = with_halo(leaf_multipoles, ((("leaf", "near"), 0),), leaf_dev)
    far_side = leaf_coupling.shape[0] // 2
    steps_out = jnp.arange(far_side, dtype=jnp.int32) + NREACH + 1
    leaf_offsets = jnp.concatenate([-steps_out, steps_out])
    slots_all = jnp.arange(leaf_dev, dtype=jnp.int32)[:, None] + leaf_dev + leaf_offsets[None, :]
    inside = ((slots_all >= 0) & (slots_all < 3 * leaf_dev)).astype(jnp.float32)
    clipped = jnp.clip(slots_all, 0, 3 * leaf_dev - 1)
    partner_rows = jnp.take(rim_moments, clipped, axis=0)
    leaf_terms = jnp.einsum(
        "lkse,kef->lksf", partner_rows, leaf_coupling.astype(jnp.float32), precision=topmost_level
    )
    leaf_nearfield = jnp.sum(leaf_terms * inside[:, :, None, None], axis=1)
    leaf_expansion = leaf_transfer.astype(jnp.float32)
    partition_moment = jnp.einsum(
        "ina,iaj->nj", leaf_multipoles, leaf_expansion, precision=topmost_level
    )
    transfer = level_transfer.astype(jnp.float32)
    coupling = level_coupling.astype(jnp.float32)
    own_coupling = node_coupling[0].astype(jnp.float32)

    def couple(height, position_index, interaction_partner):
        parity = position // (1 << height) % 2
        weight = slot_weight(parity, position_index)
        if height == 0:
            return (
                jnp.dot(interaction_partner, own_coupling[position_index], precision=topmost_level)
                * weight
            )
        return (
            jnp.dot(
                interaction_partner, coupling[height - 1, position_index], precision=topmost_level
            )
            * weight
        )

    fields_up = []
    moments = [partition_moment]
    current = partition_moment
    for height in range(1, COARSE + 1):
        sibling = swapped(current, ("leaf", "near"), height - 1)
        is_upper = position // (1 << height - 1) % 2 == 1
        lower_child = jnp.where(is_upper, sibling, current)
        upper_child = jnp.where(is_upper, current, sibling)
        current = jnp.dot(lower_child, transfer[height - 1, 0], precision=topmost_level) + jnp.dot(
            upper_child, transfer[height - 1, 1], precision=topmost_level
        )
        moments.append(current)
    for height in range(COARSE + 1):
        accum = jnp.zeros_like(partition_moment)
        for position_index, offset in enumerate(OFFSETS):
            interaction_partner = shifted(
                moments[height], ("leaf", "near"), -offset * (1 << height)
            )
            accum = accum + couple(height, position_index, interaction_partner)
        fields_up.append(accum)
    descending_fields = fields_up[COARSE]
    for height in reversed(range(COARSE)):
        parity = position // (1 << height) % 2
        chosen = jnp.where(parity == 1, transfer[height, 1], transfer[height, 0])
        descending_fields = fields_up[height] + jnp.einsum(
            "sq,rq->sr", descending_fields, chosen, precision=topmost_level
        )
    leaf_potential = (
        jnp.einsum("kb,tmb->tkm", descending_fields, leaf_expansion, precision=topmost_level)
        + leaf_nearfield
    )
    distant_sum = jnp.einsum(
        "hve,hea->hva",
        leaf_potential,
        leaf_cluster_basis.astype(jnp.float32),
        precision=topmost_level,
    )
    return distant_sum + near_sum


def solution(mesh):
    placed = (
        P(("leaf", "near"), None, None),
        P(("leaf", "near"), None, None),
        P(("leaf", "near"), None, None, None),
        P(("leaf", "near"), None),
        P(("leaf", "near"), None, None),
        P(),
        P(("leaf", "near"), None, None, None),
        P(),
        P(),
    )
    return jax.shard_map(
        local,
        mesh=mesh,
        in_specs=placed,
        out_specs=P(("leaf", "near"), None, None),
        check_vma=False,
    )
```

profile of v0, /device:TPU:1, one launch (start us, length us, event | category | flops | bytes accessed | tf_op | source)
XLA Modules:
  0.0 194.8 jit_solution(2839574984450239298)
XLA Ops:
  0.0 1.0 copy-done
  1.0 1.0 fusion.115
  2.0 1.1 convolution_bitcast_fusion.3
  3.1 8.8 %collective-permute-start.4 = (f32[32,64]{1,0:T(8,128)S(1)}, f32[32,64]{1,0:T(8,128)S(1)}, u32[]{:S(2)}, u32[]{:S(2)}) collective-permute-start(f32[32,64]{1,0:T(8,128)S(1)} %convolution_bitcast_fusion.3), channel_id=1, source_target_pairs={{0,1},{1,0},{2,3},{3,2},{4,5},{5,4},{6,7},{7,6},{8,9},{9,8},{10,11... | collective-permute-start | bytes 24584 | tf_op jit(solution)/shard_map/ppermute | solution.py:33
  11.8 10.3 %collective-permute-start.3 = (f32[32,64]{1,0:T(8,128)S(1)}, f32[32,64]{1,0:T(8,128)S(1)}, u32[]{:S(2)}, u32[]{:S(2)}) collective-permute-start(f32[32,64]{1,0:T(8,128)S(1)} %convolution_bitcast_fusion.3), channel_id=1, source_target_pairs={{0,509},{1,510},{2,511},{3,0},{4,1},{5,2},{6,3},{7,4},{8,5},{9,6},... | collective-permute-start | bytes 24584 | tf_op jit(solution)/shard_map/ppermute | solution.py:39
  22.1 2.2 %collective-permute-start.2 = (f32[32,64]{1,0:T(8,128)S(1)}, f32[32,64]{1,0:T(8,128)S(1)}, u32[]{:S(2)}, u32[]{:S(2)}) collective-permute-start(f32[32,64]{1,0:T(8,128)S(1)} %convolution_bitcast_fusion.3), channel_id=1, source_target_pairs={{0,510},{1,511},{2,0},{3,1},{4,2},{5,3},{6,4},{7,5},{8,6},{9,7},{1... | collective-permute-start | bytes 24584 | tf_op jit(solution)/shard_map/ppermute | solution.py:39
  24.3 3.1 %collective-permute-start.1 = (f32[32,64]{1,0:T(8,128)S(1)}, f32[32,64]{1,0:T(8,128)S(1)}, u32[]{:S(2)}, u32[]{:S(2)}) collective-permute-start(f32[32,64]{1,0:T(8,128)S(1)} %convolution_bitcast_fusion.3), channel_id=1, source_target_pairs={{0,2},{1,3},{2,4},{3,5},{4,6},{5,7},{6,8},{7,9},{8,10},{9,11},{10,... | collective-permute-start | bytes 24584 | tf_op jit(solution)/shard_map/ppermute | solution.py:39
  27.4 3.5 %collective-permute-start = (f32[32,64]{1,0:T(8,128)S(1)}, f32[32,64]{1,0:T(8,128)S(1)}, u32[]{:S(2)}, u32[]{:S(2)}) collective-permute-start(f32[32,64]{1,0:T(8,128)S(1)} %convolution_bitcast_fusion.3), channel_id=1, source_target_pairs={{0,3},{1,4},{2,5},{3,6},{4,7},{5,8},{6,9},{7,10},{8,11},{9,12},{10... | collective-permute-start | bytes 24584 | tf_op jit(solution)/shard_map/ppermute | solution.py:39
  31.2 0.9 fusion.114
  33.0 0.9 convert_element_type.47
  34.1 2.5 %collective-permute-start.19 = (f32[4,32,64]{2,1,0:T(8,128)S(1)}, f32[4,32,64]{2,1,0:T(8,128)S(1)}, u32[]{:S(2)}, u32[]{:S(2)}) collective-permute-start(f32[4,32,64]{2,1,0:T(8,128)S(1)} %fusion.115), channel_id=1, source_target_pairs={{0,1},{1,2},{2,3},{3,4},{4,5},{5,6},{6,7},{7,8},{8,9},{9,10},{10,1... | collective-permute-start | bytes 98312 | tf_op jit(solution)/shard_map/ppermute | solution.py:21
  37.4 0.9 convolution_add_fusion.3
  38.2 1.9 collective-permute-start.20
  41.0 3.6 %collective-permute-start.21 = (bf16[3,32,256]{2,1,0:T(8,128)(2,1)S(1)}, bf16[3,32,256]{2,1,0:T(8,128)(2,1)S(1)}, u32[]{:S(2)}, u32[]{:S(2)}) collective-permute-start(bf16[3,32,256]{2,1,0:T(8,128)(2,1)S(1)} %get-tuple-element.7), channel_id=1, source_target_pairs={{0,1},{1,2},{2,3},{3,4},{4,5},{5,6},{6,7},{7,8},{8,9},{9,10},{10,1... | collective-permute-start | bytes 147464 | tf_op jit(solution)/shard_map/ppermute | solution.py:21
  45.5 1.9 collective-permute-start.9
  48.3 1.7 collective-permute-done.9
  50.0 13.7 %collective-permute-start.7 = (f32[32,64]{1,0:T(8,128)S(1)}, f32[32,64]{1,0:T(8,128)S(1)}, u32[]{:S(2)}, u32[]{:S(2)}) collective-permute-start(f32[32,64]{1,0:T(8,128)S(1)} %convolution_add_fusion.3), channel_id=1, source_target_pairs={{0,508},{1,509},{2,510},{3,511},{4,0},{5,1},{6,2},{7,3},{8,4},{9,5... | collective-permute-start | bytes 24584 | tf_op jit(solution)/shard_map/ppermute | solution.py:39
  64.5 0.9 convolution_add_fusion.2
  65.4 1.9 collective-permute-start.6
  68.2 8.0 %collective-permute-done.6 = f32[32,64]{1,0:T(8,128)S(1)} collective-permute-done((f32[32,64]{1,0:T(8,128)S(1)}, f32[32,64]{1,0:T(8,128)S(1)}, u32[]{:S(2)}, u32[]{:S(2)}) %collective-permute-start.6) | collective-permute-done | bytes 8224 | tf_op jit(solution)/shard_map/ppermute | solution.py:39
  76.2 3.4 %collective-permute-start.8 = (f32[32,64]{1,0:T(8,128)S(1)}, f32[32,64]{1,0:T(8,128)S(1)}, u32[]{:S(2)}, u32[]{:S(2)}) collective-permute-start(f32[32,64]{1,0:T(8,128)S(1)} %convolution_add_fusion.3), channel_id=1, source_target_pairs={{0,506},{1,507},{2,508},{3,509},{4,510},{5,511},{6,0},{7,1},{8,2},... | collective-permute-start | bytes 24584 | tf_op jit(solution)/shard_map/ppermute | solution.py:39
  80.5 2.0 %collective-permute-done.8 = f32[32,64]{1,0:T(8,128)S(1)} collective-permute-done((f32[32,64]{1,0:T(8,128)S(1)}, f32[32,64]{1,0:T(8,128)S(1)}, u32[]{:S(2)}, u32[]{:S(2)}) %collective-permute-start.8) | collective-permute-done | bytes 8224 | tf_op jit(solution)/shard_map/ppermute | solution.py:39
  82.5 2.5 %collective-permute-start.14 = (f32[32,64]{1,0:T(8,128)S(1)}, f32[32,64]{1,0:T(8,128)S(1)}, u32[]{:S(2)}, u32[]{:S(2)}) collective-permute-start(f32[32,64]{1,0:T(8,128)S(1)} %convolution_add_fusion.2), channel_id=1, source_target_pairs={{0,4},{1,5},{2,6},{3,7},{4,0},{5,1},{6,2},{7,3},{8,12},{9,13},{10,... | collective-permute-start | bytes 24584 | tf_op jit(solution)/shard_map/ppermute | solution.py:33
  85.0 0.8 convolution_multiply_fusion.4
  85.8 2.0 %collective-permute-done.14 = f32[32,64]{1,0:T(8,128)S(1)} collective-permute-done((f32[32,64]{1,0:T(8,128)S(1)}, f32[32,64]{1,0:T(8,128)S(1)}, u32[]{:S(2)}, u32[]{:S(2)}) %collective-permute-start.14) | collective-permute-done | bytes 8224 | tf_op jit(solution)/shard_map/ppermute | solution.py:33
  87.9 9.1 %collective-permute-start.12 = (f32[32,64]{1,0:T(8,128)S(1)}, f32[32,64]{1,0:T(8,128)S(1)}, u32[]{:S(2)}, u32[]{:S(2)}) collective-permute-start(f32[32,64]{1,0:T(8,128)S(1)} %convolution_add_fusion.2), channel_id=1, source_target_pairs={{0,504},{1,505},{2,506},{3,507},{4,508},{5,509},{6,510},{7,511},{8... | collective-permute-start | bytes 24584 | tf_op jit(solution)/shard_map/ppermute | solution.py:39
  97.8 0.9 convolution_add_fusion.1
  98.7 2.5 %collective-permute-start.11 = (f32[32,64]{1,0:T(8,128)S(1)}, f32[32,64]{1,0:T(8,128)S(1)}, u32[]{:S(2)}, u32[]{:S(2)}) collective-permute-start(f32[32,64]{1,0:T(8,128)S(1)} %convolution_add_fusion.2), channel_id=1, source_target_pairs={{0,8},{1,9},{2,10},{3,11},{4,12},{5,13},{6,14},{7,15},{8,16},{9,17... | collective-permute-start | bytes 24584 | tf_op jit(solution)/shard_map/ppermute | solution.py:39
  102.1 9.6 %collective-permute-done.11 = f32[32,64]{1,0:T(8,128)S(1)} collective-permute-done((f32[32,64]{1,0:T(8,128)S(1)}, f32[32,64]{1,0:T(8,128)S(1)}, u32[]{:S(2)}, u32[]{:S(2)}) %collective-permute-start.11) | collective-permute-done | bytes 8224 | tf_op jit(solution)/shard_map/ppermute | solution.py:39
  111.6 2.9 %collective-permute-start.13 = (f32[32,64]{1,0:T(8,128)S(1)}, f32[32,64]{1,0:T(8,128)S(1)}, u32[]{:S(2)}, u32[]{:S(2)}) collective-permute-start(f32[32,64]{1,0:T(8,128)S(1)} %convolution_add_fusion.2), channel_id=1, source_target_pairs={{0,500},{1,501},{2,502},{3,503},{4,504},{5,505},{6,506},{7,507},{8... | collective-permute-start | bytes 24584 | tf_op jit(solution)/shard_map/ppermute | solution.py:39
  115.4 2.8 %collective-permute-done.13 = f32[32,64]{1,0:T(8,128)S(1)} collective-permute-done((f32[32,64]{1,0:T(8,128)S(1)}, f32[32,64]{1,0:T(8,128)S(1)}, u32[]{:S(2)}, u32[]{:S(2)}) %collective-permute-start.13) | collective-permute-done | bytes 8224 | tf_op jit(solution)/shard_map/ppermute | solution.py:39
  118.2 3.5 %collective-permute-start.17 = (f32[32,64]{1,0:T(8,128)S(1)}, f32[32,64]{1,0:T(8,128)S(1)}, u32[]{:S(2)}, u32[]{:S(2)}) collective-permute-start(f32[32,64]{1,0:T(8,128)S(1)} %convolution_add_fusion.1), channel_id=1, source_target_pairs={{0,496},{1,497},{2,498},{3,499},{4,500},{5,501},{6,502},{7,503},{8... | collective-permute-start | bytes 24584 | tf_op jit(solution)/shard_map/ppermute | solution.py:39
  122.7 1.9 collective-permute-start.16
  125.4 5.1 %collective-permute-done.16 = f32[32,64]{1,0:T(8,128)S(1)} collective-permute-done((f32[32,64]{1,0:T(8,128)S(1)}, f32[32,64]{1,0:T(8,128)S(1)}, u32[]{:S(2)}, u32[]{:S(2)}) %collective-permute-start.16) | collective-permute-done | bytes 8224 | tf_op jit(solution)/shard_map/ppermute | solution.py:39
  130.6 10.3 %collective-permute-start.18 = (f32[32,64]{1,0:T(8,128)S(1)}, f32[32,64]{1,0:T(8,128)S(1)}, u32[]{:S(2)}, u32[]{:S(2)}) collective-permute-start(f32[32,64]{1,0:T(8,128)S(1)} %convolution_add_fusion.1), channel_id=1, source_target_pairs={{0,488},{1,489},{2,490},{3,491},{4,492},{5,493},{6,494},{7,495},{8... | collective-permute-start | bytes 24584 | tf_op jit(solution)/shard_map/ppermute | solution.py:39
  141.7 5.4 %collective-permute-start.15 = (f32[32,64]{1,0:T(8,128)S(1)}, f32[32,64]{1,0:T(8,128)S(1)}, u32[]{:S(2)}, u32[]{:S(2)}) collective-permute-start(f32[32,64]{1,0:T(8,128)S(1)} %convolution_add_fusion.1), channel_id=1, source_target_pairs={{0,24},{1,25},{2,26},{3,27},{4,28},{5,29},{6,30},{7,31},{8,32},{9,... | collective-permute-start | bytes 24584 | tf_op jit(solution)/shard_map/ppermute | solution.py:39
  148.0 6.9 %collective-permute-done.15 = f32[32,64]{1,0:T(8,128)S(1)} collective-permute-done((f32[32,64]{1,0:T(8,128)S(1)}, f32[32,64]{1,0:T(8,128)S(1)}, u32[]{:S(2)}, u32[]{:S(2)}) %collective-permute-start.15) | collective-permute-done | bytes 8224 | tf_op jit(solution)/shard_map/ppermute | solution.py:39
  154.9 7.6 %collective-permute-start.10 = (f32[32,64]{1,0:T(8,128)S(1)}, f32[32,64]{1,0:T(8,128)S(1)}, u32[]{:S(2)}, u32[]{:S(2)}) collective-permute-start(f32[32,64]{1,0:T(8,128)S(1)} %convolution_add_fusion.2), channel_id=1, source_target_pairs={{0,12},{1,13},{2,14},{3,15},{4,16},{5,17},{6,18},{7,19},{8,20},{9,... | collective-permute-start | bytes 24584 | tf_op jit(solution)/shard_map/ppermute | solution.py:39
  162.4 0.9 fusion.5
  163.5 1.0 collective-permute-done.10
  164.4 4.9 %collective-permute-start.5 = (f32[32,64]{1,0:T(8,128)S(1)}, f32[32,64]{1,0:T(8,128)S(1)}, u32[]{:S(2)}, u32[]{:S(2)}) collective-permute-start(f32[32,64]{1,0:T(8,128)S(1)} %convolution_add_fusion.3), channel_id=1, source_target_pairs={{0,6},{1,7},{2,8},{3,9},{4,10},{5,11},{6,12},{7,13},{8,14},{9,15},... | collective-permute-start | bytes 24584 | tf_op jit(solution)/shard_map/ppermute | solution.py:39
  169.3 0.9 fusion.9
  170.3 5.9 %collective-permute-done.5 = f32[32,64]{1,0:T(8,128)S(1)} collective-permute-done((f32[32,64]{1,0:T(8,128)S(1)}, f32[32,64]{1,0:T(8,128)S(1)}, u32[]{:S(2)}, u32[]{:S(2)}) %collective-permute-start.5) | collective-permute-done | bytes 8224 | tf_op jit(solution)/shard_map/ppermute | solution.py:39
  176.2 10.5 %collective-permute-start.22 = (bf16[3,32,256]{2,1,0:T(8,128)(2,1)S(1)}, bf16[3,32,256]{2,1,0:T(8,128)(2,1)S(1)}, u32[]{:S(2)}, u32[]{:S(2)}) collective-permute-start(bf16[3,32,256]{2,1,0:T(8,128)(2,1)S(1)} %get-tuple-element.8), channel_id=1, source_target_pairs={{1,0},{2,1},{3,2},{4,3},{5,4},{6,5},{7,6},{8,7},{9,8},{10,9},{11,1... | collective-permute-start | bytes 147464 | tf_op jit(solution)/shard_map/ppermute | solution.py:23
  186.7 0.9 fusion.13
  188.9 0.9 fusion.18
  190.7 3.2 %convolution_bitcast_fusion.1 = f32[4,32,256]{2,1,0:T(8,128)S(1)} fusion(bf16[4,7,256,256]{3,2,1,0:T(8,128)(2,1)} %param.11, bf16[4,7,32,256]{3,2,1,0:T(8,128)(2,1)S(1)} %bitcast.129, pred[4,7]{1,0:T(4,128)(4,1)S(1)} %get-tuple-element.5), kind=kOutput, calls=%fused_computation.6 | convolution fusion | flops 117669888 | bytes 4259868 | tf_op jit(solution)/shard_map/lkpq,lksq->lsp/dot_general | solution.py:67
  193.9 0.9 convolution_add_fusion
  (53 shorter events, 15.7 us)
Async XLA Ops:
  0.0 1.0 copy-start
  0.0 190.1 %copy-start.1 = (bf16[4,32,256]{2,1,0:T(8,128)(2,1)S(1)}, bf16[4,32,256]{2,1,0:T(8,128)(2,1)}, u32[]{:S(2)}) copy-start(bf16[4,32,256]{2,1,0:T(8,128)(2,1)} %param.9) | copy-start | bytes 196612
  0.0 189.7 %copy-start.2 = (bf16[4,64,64]{2,1,0:T(8,128)(2,1)S(1)}, bf16[4,64,64]{2,1,0:T(8,128)(2,1)}, u32[]{:S(2)}) copy-start(bf16[4,64,64]{2,1,0:T(8,128)(2,1)} %param.13) | copy-start | bytes 98308
  0.0 188.4 %copy-start.3 = (bf16[8,64,64]{2,1,0:T(8,128)(2,1)S(1)}, bf16[8,64,64]{2,1,0:T(8,128)(2,1)}, u32[]{:S(2)}) copy-start(bf16[8,64,64]{2,1,0:T(8,128)(2,1)} %param.14) | copy-start | bytes 196612
  3.1 31.0 %collective-permute-start.4 = (f32[32,64]{1,0:T(8,128)S(1)}, f32[32,64]{1,0:T(8,128)S(1)}, u32[]{:S(2)}, u32[]{:S(2)}) collective-permute-start(f32[32,64]{1,0:T(8,128)S(1)} %convolution_bitcast_fusion.3), channel_id=1, source_target_pairs={{0,1},{1,0},{2,3},{3,2},{4,5},{5,4},{6,7},{7,6},{8,9},{9,8},{10,11... | collective-permute-start | bytes 24584 | tf_op jit(solution)/shard_map/ppermute | solution.py:33
  11.8 33.7 %collective-permute-start.3 = (f32[32,64]{1,0:T(8,128)S(1)}, f32[32,64]{1,0:T(8,128)S(1)}, u32[]{:S(2)}, u32[]{:S(2)}) collective-permute-start(f32[32,64]{1,0:T(8,128)S(1)} %convolution_bitcast_fusion.3), channel_id=1, source_target_pairs={{0,509},{1,510},{2,511},{3,0},{4,1},{5,2},{6,3},{7,4},{8,5},{9,6},... | collective-permute-start | bytes 24584 | tf_op jit(solution)/shard_map/ppermute | solution.py:39
  22.1 16.1 %collective-permute-start.2 = (f32[32,64]{1,0:T(8,128)S(1)}, f32[32,64]{1,0:T(8,128)S(1)}, u32[]{:S(2)}, u32[]{:S(2)}) collective-permute-start(f32[32,64]{1,0:T(8,128)S(1)} %convolution_bitcast_fusion.3), channel_id=1, source_target_pairs={{0,510},{1,511},{2,0},{3,1},{4,2},{5,3},{6,4},{7,5},{8,6},{9,7},{1... | collective-permute-start | bytes 24584 | tf_op jit(solution)/shard_map/ppermute | solution.py:39
  24.3 16.7 %collective-permute-start.1 = (f32[32,64]{1,0:T(8,128)S(1)}, f32[32,64]{1,0:T(8,128)S(1)}, u32[]{:S(2)}, u32[]{:S(2)}) collective-permute-start(f32[32,64]{1,0:T(8,128)S(1)} %convolution_bitcast_fusion.3), channel_id=1, source_target_pairs={{0,2},{1,3},{2,4},{3,5},{4,6},{5,7},{6,8},{7,9},{8,10},{9,11},{10,... | collective-permute-start | bytes 24584 | tf_op jit(solution)/shard_map/ppermute | solution.py:39
  27.4 161.4 %collective-permute-start = (f32[32,64]{1,0:T(8,128)S(1)}, f32[32,64]{1,0:T(8,128)S(1)}, u32[]{:S(2)}, u32[]{:S(2)}) collective-permute-start(f32[32,64]{1,0:T(8,128)S(1)} %convolution_bitcast_fusion.3), channel_id=1, source_target_pairs={{0,3},{1,4},{2,5},{3,6},{4,7},{5,8},{6,9},{7,10},{8,11},{9,12},{10... | collective-permute-start | bytes 24584 | tf_op jit(solution)/shard_map/ppermute | solution.py:39
  34.1 153.7 %collective-permute-start.19 = (f32[4,32,64]{2,1,0:T(8,128)S(1)}, f32[4,32,64]{2,1,0:T(8,128)S(1)}, u32[]{:S(2)}, u32[]{:S(2)}) collective-permute-start(f32[4,32,64]{2,1,0:T(8,128)S(1)} %fusion.115), channel_id=1, source_target_pairs={{0,1},{1,2},{2,3},{3,4},{4,5},{5,6},{6,7},{7,8},{8,9},{9,10},{10,1... | collective-permute-start | bytes 98312 | tf_op jit(solution)/shard_map/ppermute | solution.py:21
  38.2 149.5 %collective-permute-start.20 = (f32[4,32,64]{2,1,0:T(8,128)S(1)}, f32[4,32,64]{2,1,0:T(8,128)S(1)}, u32[]{:S(2)}, u32[]{:S(2)}) collective-permute-start(f32[4,32,64]{2,1,0:T(8,128)S(1)} %fusion.115), channel_id=1, source_target_pairs={{1,0},{2,1},{3,2},{4,3},{5,4},{6,5},{7,6},{8,7},{9,8},{10,9},{11,1... | collective-permute-start | bytes 98312 | tf_op jit(solution)/shard_map/ppermute | solution.py:23
  41.0 149.0 %collective-permute-start.21 = (bf16[3,32,256]{2,1,0:T(8,128)(2,1)S(1)}, bf16[3,32,256]{2,1,0:T(8,128)(2,1)S(1)}, u32[]{:S(2)}, u32[]{:S(2)}) collective-permute-start(bf16[3,32,256]{2,1,0:T(8,128)(2,1)S(1)} %get-tuple-element.7), channel_id=1, source_target_pairs={{0,1},{1,2},{2,3},{3,4},{4,5},{5,6},{6,7},{7,8},{8,9},{9,10},{10,1... | collective-permute-start | bytes 147464 | tf_op jit(solution)/shard_map/ppermute | solution.py:21
  45.5 4.5 %collective-permute-start.9 = (f32[32,64]{1,0:T(8,128)S(1)}, f32[32,64]{1,0:T(8,128)S(1)}, u32[]{:S(2)}, u32[]{:S(2)}) collective-permute-start(f32[32,64]{1,0:T(8,128)S(1)} %convolution_add_fusion.3), channel_id=1, source_target_pairs={{0,2},{1,3},{2,0},{3,1},{4,6},{5,7},{6,4},{7,5},{8,10},{9,11},{10,... | collective-permute-start | bytes 24584 | tf_op jit(solution)/shard_map/ppermute | solution.py:33
  50.0 15.4 %collective-permute-start.7 = (f32[32,64]{1,0:T(8,128)S(1)}, f32[32,64]{1,0:T(8,128)S(1)}, u32[]{:S(2)}, u32[]{:S(2)}) collective-permute-start(f32[32,64]{1,0:T(8,128)S(1)} %convolution_add_fusion.3), channel_id=1, source_target_pairs={{0,508},{1,509},{2,510},{3,511},{4,0},{5,1},{6,2},{7,3},{8,4},{9,5... | collective-permute-start | bytes 24584 | tf_op jit(solution)/shard_map/ppermute | solution.py:39
  65.4 10.8 %collective-permute-start.6 = (f32[32,64]{1,0:T(8,128)S(1)}, f32[32,64]{1,0:T(8,128)S(1)}, u32[]{:S(2)}, u32[]{:S(2)}) collective-permute-start(f32[32,64]{1,0:T(8,128)S(1)} %convolution_add_fusion.3), channel_id=1, source_target_pairs={{0,4},{1,5},{2,6},{3,7},{4,8},{5,9},{6,10},{7,11},{8,12},{9,13},{1... | collective-permute-start | bytes 24584 | tf_op jit(solution)/shard_map/ppermute | solution.py:39
  76.2 6.3 %collective-permute-start.8 = (f32[32,64]{1,0:T(8,128)S(1)}, f32[32,64]{1,0:T(8,128)S(1)}, u32[]{:S(2)}, u32[]{:S(2)}) collective-permute-start(f32[32,64]{1,0:T(8,128)S(1)} %convolution_add_fusion.3), channel_id=1, source_target_pairs={{0,506},{1,507},{2,508},{3,509},{4,510},{5,511},{6,0},{7,1},{8,2},... | collective-permute-start | bytes 24584 | tf_op jit(solution)/shard_map/ppermute | solution.py:39
  82.5 5.4 %collective-permute-start.14 = (f32[32,64]{1,0:T(8,128)S(1)}, f32[32,64]{1,0:T(8,128)S(1)}, u32[]{:S(2)}, u32[]{:S(2)}) collective-permute-start(f32[32,64]{1,0:T(8,128)S(1)} %convolution_add_fusion.2), channel_id=1, source_target_pairs={{0,4},{1,5},{2,6},{3,7},{4,0},{5,1},{6,2},{7,3},{8,12},{9,13},{10,... | collective-permute-start | bytes 24584 | tf_op jit(solution)/shard_map/ppermute | solution.py:33
  87.9 10.8 %collective-permute-start.12 = (f32[32,64]{1,0:T(8,128)S(1)}, f32[32,64]{1,0:T(8,128)S(1)}, u32[]{:S(2)}, u32[]{:S(2)}) collective-permute-start(f32[32,64]{1,0:T(8,128)S(1)} %convolution_add_fusion.2), channel_id=1, source_target_pairs={{0,504},{1,505},{2,506},{3,507},{4,508},{5,509},{6,510},{7,511},{8... | collective-permute-start | bytes 24584 | tf_op jit(solution)/shard_map/ppermute | solution.py:39
  98.7 12.9 %collective-permute-start.11 = (f32[32,64]{1,0:T(8,128)S(1)}, f32[32,64]{1,0:T(8,128)S(1)}, u32[]{:S(2)}, u32[]{:S(2)}) collective-permute-start(f32[32,64]{1,0:T(8,128)S(1)} %convolution_add_fusion.2), channel_id=1, source_target_pairs={{0,8},{1,9},{2,10},{3,11},{4,12},{5,13},{6,14},{7,15},{8,16},{9,17... | collective-permute-start | bytes 24584 | tf_op jit(solution)/shard_map/ppermute | solution.py:39
  111.6 6.6 %collective-permute-start.13 = (f32[32,64]{1,0:T(8,128)S(1)}, f32[32,64]{1,0:T(8,128)S(1)}, u32[]{:S(2)}, u32[]{:S(2)}) collective-permute-start(f32[32,64]{1,0:T(8,128)S(1)} %convolution_add_fusion.2), channel_id=1, source_target_pairs={{0,500},{1,501},{2,502},{3,503},{4,504},{5,505},{6,506},{7,507},{8... | collective-permute-start | bytes 24584 | tf_op jit(solution)/shard_map/ppermute | solution.py:39
  118.2 4.5 %collective-permute-start.17 = (f32[32,64]{1,0:T(8,128)S(1)}, f32[32,64]{1,0:T(8,128)S(1)}, u32[]{:S(2)}, u32[]{:S(2)}) collective-permute-start(f32[32,64]{1,0:T(8,128)S(1)} %convolution_add_fusion.1), channel_id=1, source_target_pairs={{0,496},{1,497},{2,498},{3,499},{4,500},{5,501},{6,502},{7,503},{8... | collective-permute-start | bytes 24584 | tf_op jit(solution)/shard_map/ppermute | solution.py:39
  122.7 7.9 %collective-permute-start.16 = (f32[32,64]{1,0:T(8,128)S(1)}, f32[32,64]{1,0:T(8,128)S(1)}, u32[]{:S(2)}, u32[]{:S(2)}) collective-permute-start(f32[32,64]{1,0:T(8,128)S(1)} %convolution_add_fusion.1), channel_id=1, source_target_pairs={{0,16},{1,17},{2,18},{3,19},{4,20},{5,21},{6,22},{7,23},{8,24},{9,... | collective-permute-start | bytes 24584 | tf_op jit(solution)/shard_map/ppermute | solution.py:39
  130.6 11.1 %collective-permute-start.18 = (f32[32,64]{1,0:T(8,128)S(1)}, f32[32,64]{1,0:T(8,128)S(1)}, u32[]{:S(2)}, u32[]{:S(2)}) collective-permute-start(f32[32,64]{1,0:T(8,128)S(1)} %convolution_add_fusion.1), channel_id=1, source_target_pairs={{0,488},{1,489},{2,490},{3,491},{4,492},{5,493},{6,494},{7,495},{8... | collective-permute-start | bytes 24584 | tf_op jit(solution)/shard_map/ppermute | solution.py:39
  141.7 13.1 %collective-permute-start.15 = (f32[32,64]{1,0:T(8,128)S(1)}, f32[32,64]{1,0:T(8,128)S(1)}, u32[]{:S(2)}, u32[]{:S(2)}) collective-permute-start(f32[32,64]{1,0:T(8,128)S(1)} %convolution_add_fusion.1), channel_id=1, source_target_pairs={{0,24},{1,25},{2,26},{3,27},{4,28},{5,29},{6,30},{7,31},{8,32},{9,... | collective-permute-start | bytes 24584 | tf_op jit(solution)/shard_map/ppermute | solution.py:39
  154.9 9.6 %collective-permute-start.10 = (f32[32,64]{1,0:T(8,128)S(1)}, f32[32,64]{1,0:T(8,128)S(1)}, u32[]{:S(2)}, u32[]{:S(2)}) collective-permute-start(f32[32,64]{1,0:T(8,128)S(1)} %convolution_add_fusion.2), channel_id=1, source_target_pairs={{0,12},{1,13},{2,14},{3,15},{4,16},{5,17},{6,18},{7,19},{8,20},{9,... | collective-permute-start | bytes 24584 | tf_op jit(solution)/shard_map/ppermute | solution.py:39
  164.4 11.8 %collective-permute-start.5 = (f32[32,64]{1,0:T(8,128)S(1)}, f32[32,64]{1,0:T(8,128)S(1)}, u32[]{:S(2)}, u32[]{:S(2)}) collective-permute-start(f32[32,64]{1,0:T(8,128)S(1)} %convolution_add_fusion.3), channel_id=1, source_target_pairs={{0,6},{1,7},{2,8},{3,9},{4,10},{5,11},{6,12},{7,13},{8,14},{9,15},... | collective-permute-start | bytes 24584 | tf_op jit(solution)/shard_map/ppermute | solution.py:39
  176.2 13.8 %collective-permute-start.22 = (bf16[3,32,256]{2,1,0:T(8,128)(2,1)S(1)}, bf16[3,32,256]{2,1,0:T(8,128)(2,1)S(1)}, u32[]{:S(2)}, u32[]{:S(2)}) collective-permute-start(bf16[3,32,256]{2,1,0:T(8,128)(2,1)S(1)} %get-tuple-element.8), channel_id=1, source_target_pairs={{1,0},{2,1},{3,2},{4,3},{5,4},{6,5},{7,6},{8,7},{9,8},{10,9},{11,1... | collective-permute-start | bytes 147464 | tf_op jit(solution)/shard_map/ppermute | solution.py:23
where the time goes:
time: 198 us; the launch traced here: 195 us
  starting transfers between devices  118 us (60%)
  waiting for transfers between devices  45.3 us (23%)
  matrix products  26 us (13%)
  local copies, waits for them, and re-layouts  3.3 us (2%)
    ppermute x16, starting transfers between devices, shifted(): return lax.ppermute(value, axis, pairs)  86.1 us
    ppermute x16, waiting for transfers between devices, shifted(): return lax.ppermute(value, axis, pairs)  41.5 us
    ppermute x3, starting transfers between devices, swapped(): return lax.ppermute(value, axis, pairs)  13.2 us
    ppermute x2, starting transfers between devices, with_halo(): lax.ppermute(head, axis, [((i + 1) % count, i) for i in range(count)])  12.4 us
    dot_general x12, matrix products, couple(): jnp.dot(interaction_partner, coupling[height - 1, position_index], precis...  10.2 us
    ppermute x2, starting transfers between devices, with_halo(): lax.ppermute(tail, axis, [(i, (i + 1) % count) for i in range(count)])  6.1 us
  transfers between devices with their start and end apart: 23, of which 11 were waited for; matrix products, arithmetic and copies ran while one was open for 12% of the time, Pallas kernels for 0%

commit v1 on v0

v1 whole, which is shorter than its diff:
```python
import jax
import jax.numpy as jnp
from jax import lax
from jax.experimental import pallas as pl
from jax.experimental.pallas import tpu as pltpu
from jax.sharding import PartitionSpec as P

AXES = ("leaf", "near")
NREACH = 3
OFFSETS = (-3, -2, 2, 3)
CHIPS = 8
BF16, F32 = jnp.bfloat16, jnp.float32
VMEM = pl.BlockSpec(memory_space=pltpu.VMEM)
HBM = pl.BlockSpec(memory_space=pltpu.HBM)


def dot(a, b):
    return lax.dot_general(a, b, (((1,), (0,)), ((), ())), preferred_element_type=F32)


def dot_nt(a, b):
    return lax.dot_general(a, b, (((1,), (1,)), ((), ())), preferred_element_type=F32)


def halves(value):
    high = value.astype(BF16)
    low = (value - high.astype(F32)).astype(BF16)
    return jnp.concatenate([high, low], axis=1)


def stacked(weights, axis):
    return jnp.concatenate([w for w in weights for _ in range(2)], axis=axis)


def load(sources, targets, semaphores):
    copies = [
        pltpu.make_async_copy(source, target, semaphores.at[i])
        for i, (source, target) in enumerate(zip(sources, targets, strict=True))
    ]
    for copy in copies:
        copy.start()
    return copies


def moments_kernel(
    x_hbm, basis_hbm, transfer_hbm, x_ref, basis_ref, transfer_ref, package_ref, semaphores
):
    odd = lax.axis_index("near") % 2
    copies = load(
        (x_hbm, basis_hbm, transfer_hbm), (x_ref, basis_ref, transfer_ref), semaphores
    )
    copies[0].wait()
    package_ref[0:3] = x_ref[pl.ds(1 - odd, 3)]
    copies[1].wait()
    parts = [halves(dot_nt(x_ref[j], basis_ref[j])) for j in range(4)]
    package_ref[3] = jnp.concatenate(parts[:2], axis=1)
    package_ref[4] = jnp.concatenate(parts[2:], axis=1)
    copies[2].wait()
    weights = stacked([transfer_ref[j] for j in range(4)], 0)
    node = halves(dot(jnp.concatenate(parts, axis=1), weights))
    package_ref[5] = jnp.concatenate([node, jnp.zeros_like(node)], axis=1)


def weights_kernel(
    level_hbm, coupling_hbm, leaf_hbm, node_hbm, up_ref, down_ref, coupling_ref, leaf_ref, node_ref,
    level, coupling, leaf, node, semaphores,
):
    near = lax.axis_index("near")
    copies = load(
        (level_hbm, coupling_hbm, leaf_hbm, node_hbm), (level, coupling, leaf, node), semaphores
    )
    copies[0].wait()
    for c in range(3):
        up_ref[c] = stacked([level[c, 0], level[c, 1]], 0)
        down_ref[c] = stacked([level[c, (near >> c) % 2]], 1)
    copies[1].wait()
    for c in range(3):
        coupling_ref[c] = stacked([coupling[c, k] for k in range(4)], 0)
    copies[2].wait()
    leaf_ref[...] = stacked([leaf[k] for k in range(8)], 0)
    copies[3].wait()
    node_ref[...] = stacked([node[0, k] for k in range(4)], 0)


def pair_kernel(x_ref, mine_ref, sibling_ref, up_ref, chunk_ref, next_ref, nodes_ref):
    odd = lax.axis_index("near") % 2
    mine = mine_ref[5][:, :128]
    sibling = sibling_ref[5][:, :128]
    even_node = jnp.where(odd == 1, sibling, mine)
    odd_node = jnp.where(odd == 1, mine, sibling)
    chip = halves(dot(jnp.concatenate([even_node, odd_node], axis=1), up_ref[0]))
    for j in range(chunk_ref.shape[0]):
        chunk_ref[j] = chip
    nodes_ref[...] = jnp.concatenate([mine, sibling], axis=1)
    next_ref[0:3] = x_ref[pl.ds(odd, 3)]
    next_ref[3:5] = mine_ref[3:5]
    next_ref[5] = jnp.concatenate([sibling, sibling], axis=1)


def levels_kernel(
    chips_ref, up_ref, down_ref, coupling_ref, send_ref, own_ref, quads, octets
):
    near = lax.axis_index("near")
    side = lax.axis_index("leaf") % 2
    z = near // 2
    rows = [jnp.concatenate([chips_ref[2 * q], chips_ref[2 * q + 1]], axis=1) for q in range(8)]
    second = halves(dot(jnp.concatenate(rows, axis=0), up_ref[1])).reshape(8, 32, 128)
    quads[...] = second
    rows = [jnp.concatenate([second[2 * q], second[2 * q + 1]], axis=1) for q in range(4)]
    third = halves(dot(jnp.concatenate(rows, axis=0), up_ref[2])).reshape(4, 32, 128)
    octets[...] = third
    own = side * CHIPS + z
    other = jnp.where(side == 0, z - CHIPS, z + 2 * CHIPS)
    fields = []
    for c, table in ((0, chips_ref), (1, quads), (2, octets)):
        count = table.shape[0]
        parity = (z >> c) % 2
        rows = []
        for target in (own, other):
            node = target >> c
            blocks = []
            for k, offset in enumerate(OFFSETS):
                partner = node + offset
                valid = (partner >= 0) & (partner < count)
                if k == 0:
                    valid = valid & (parity == 1)
                if k == 3:
                    valid = valid & (parity == 0)
                block = table[jnp.clip(partner, 0, count - 1)]
                blocks.append(jnp.where(valid, block, jnp.zeros_like(block)))
            rows.append(jnp.concatenate(blocks, axis=1))
        fields.append(dot(jnp.concatenate(rows, axis=0), coupling_ref[c]))
    field = fields[2]
    for c in (2, 1, 0):
        field = dot_nt(halves(field), down_ref[c])
        if c:
            field = field + fields[c - 1]
    own_ref[...] = field[:32]
    send_ref[...] = halves(field[32:])


def near_kernel(
    x_ref, sibling_ref, next_ref, nodes_ref, own_ref, leaf_ref, node_ref, cols_hbm, blocks_hbm,
    near_ref, far_ref, field_ref, window, cols, blocks, semaphores,
):
    copies = load(
        [blocks_hbm.at[j] for j in range(4)] + [cols_hbm],
        [blocks.at[j] for j in range(4)] + [cols],
        semaphores,
    )
    near = lax.axis_index("near")
    odd = near % 2
    first = (lax.axis_index("leaf") * (2 * CHIPS) + near) * 4 - NREACH
    is_odd = odd == 1
    window[3:7] = x_ref[...]
    window[0:3] = jnp.where(is_odd, sibling_ref[0:3], next_ref[0:3])
    window[7:10] = jnp.where(is_odd, next_ref[0:3], sibling_ref[0:3])
    zero = jnp.zeros((32, 128), BF16)
    left, right = [], []
    for pair in (3, 4):
        from_sibling, from_next = sibling_ref[pair], next_ref[pair]
        before = jnp.where(is_odd, from_sibling, from_next)
        after = jnp.where(is_odd, from_next, from_sibling)
        left += [before[:, :128], before[:, 128:]]
        right += [after[:, :128], after[:, 128:]]
    rows = []
    for j in range(4):
        row = [left[j - k] if k <= j else zero for k in range(4)]
        row += [right[j + k] if k <= 3 - j else zero for k in range(4)]
        rows.append(jnp.concatenate(row, axis=1))
    coupled = dot(jnp.concatenate(rows, axis=0), leaf_ref[...])
    for j in range(4):
        far_ref[j] = coupled[32 * j : 32 * j + 32]
    direct = nodes_ref[:, :128]
    beside = nodes_ref[:, 128:]
    adjacent = next_ref[5][:, :128]
    row = [
        jnp.where(is_odd, direct, zero),
        jnp.where(is_odd, beside, adjacent),
        jnp.where(is_odd, adjacent, beside),
        jnp.where(is_odd, zero, direct),
    ]
    field_ref[...] = own_ref[...] + dot(jnp.concatenate(row, axis=1), node_ref[...])
    copies[4].wait()
    for j in range(4):
        total = None
        copies[j].wait()
        for k in range(7):
            place = (cols[j, k] - first) & 2047
            term = dot_nt(window[place], blocks[j, k])
            total = term if total is None else total + term
        near_ref[j] = total


def product_kernel(near_ref, far_ref, field_ref, given_ref, transfer_ref, basis_ref, out_ref):
    given = given_ref[...].astype(F32)
    field = halves(field_ref[...] + given[:, :64] + given[:, 64:])
    for j in range(4):
        leaf_field = dot_nt(field, stacked([transfer_ref[j]], 1)) + far_ref[j]
        out_ref[j] = dot(halves(leaf_field), stacked([basis_ref[j]], 0)) + near_ref[j]


def call(kernel, out, specs, scratch=(), flops=0, size=0):
    return pl.pallas_call(
        kernel,
        out_shape=[jax.ShapeDtypeStruct(shape, dtype) for shape, dtype in out],
        in_specs=specs,
        out_specs=[VMEM] * len(out),
        scratch_shapes=list(scratch),
        compiler_params=pltpu.CompilerParams(vmem_limit_bytes=16 << 20),
        cost_estimate=pl.CostEstimate(flops=flops, bytes_accessed=size, transcendentals=0),
    )


def in_hbm(*arrays):
    return [pltpu.with_memory_space_constraint(array, pltpu.HBM) for array in arrays]


def permute(value, partner):
    members = lax.axis_size(AXES)
    return lax.ppermute(value, AXES, [(i, partner(i) % members) for i in range(members)])


def local(
    input_point_values,
    leaf_cluster_basis,
    near_blocks,
    near_cols,
    leaf_transfer,
    leaf_coupling,
    node_coupling,
    level_transfer,
    level_coupling,
):
    block = lax.axis_size("near")
    x, basis, transfer, package = call(
        moments_kernel,
        [((4, 32, 256), BF16), ((4, 64, 256), BF16), ((4, 64, 64), BF16), ((6, 32, 256), BF16)],
        [HBM] * 3,
        [pltpu.SemaphoreType.DMA((3,))],
    )(*in_hbm(input_point_values, leaf_cluster_basis, leaf_transfer))
    sibling = permute(package, lambda i: i ^ 1)
    up, down, coupling, leaf, node = call(
        weights_kernel,
        [
            ((3, 256, 64), BF16),
            ((3, 64, 128), BF16),
            ((3, 512, 64), BF16),
            ((1024, 64), BF16),
            ((512, 64), BF16),
        ],
        [HBM] * 4,
        [
            pltpu.VMEM((3, 2, 64, 64), BF16),
            pltpu.VMEM((3, 4, 64, 64), BF16),
            pltpu.VMEM((8, 64, 64), BF16),
            pltpu.VMEM((1, 4, 64, 64), BF16),
            pltpu.SemaphoreType.DMA((4,)),
        ],
        size=2_000_000,
    )(*in_hbm(level_transfer, level_coupling, leaf_coupling, node_coupling))
    chunk, package, nodes = call(
        pair_kernel,
        [((16, 32, 128), BF16), ((6, 32, 256), BF16), ((32, 256), BF16)],
        [VMEM] * 4,
    )(x, package, sibling, up)
    groups = [
        [2 * block * pair + block * side + 2 * z + core for side in range(2) for z in range(CHIPS)]
        for pair in range(lax.axis_size("leaf") // 2)
        for core in range(2)
    ]
    chips = lax.all_to_all(chunk, AXES, 0, 0, axis_index_groups=groups)
    after = permute(package, lambda i: i + 1 if i % 2 else i - 1)
    nodes = permute(nodes, lambda i: i - 3 if i % 2 else i + 3)
    send, own = call(
        levels_kernel,
        [((32, 128), BF16), ((32, 64), F32)],
        [VMEM] * 4,
        [pltpu.VMEM((8, 32, 128), BF16), pltpu.VMEM((4, 32, 128), BF16)],
    )(chips, up, down, coupling)
    given = permute(send, lambda i: i + block if i // block % 2 else i - block)
    near, far, field = call(
        near_kernel,
        [((4, 32, 256), F32), ((4, 32, 64), F32), ((32, 64), F32)],
        [VMEM] * 7 + [HBM] * 2,
        [
            pltpu.VMEM((10, 32, 256), BF16),
            pltpu.SMEM((4, 7), jnp.int32),
            pltpu.VMEM((4, 7, 256, 256), BF16),
            pltpu.SemaphoreType.DMA((5,)),
        ],
        flops=200_000_000,
        size=4_000_000,
    )(x, sibling, after, nodes, own, leaf, node, *in_hbm(near_cols, near_blocks))
    (out,) = call(product_kernel, [((4, 32, 256), F32)], [VMEM] * 6)(
        near, far, field, given, transfer, basis
    )
    return out


def solution(mesh):
    spread = P(AXES)
    placed = (spread, spread, spread, spread, spread, P(), spread, P(), P())
    return jax.shard_map(
        local, mesh=mesh, in_specs=placed, out_specs=spread, check_vma=False
    )
```

time: 198 us -> 41.4 us (0.21); the launches traced: 195 us -> 41.1 us
  starting transfers between devices: 118 us -> 29.6 us
  waiting for transfers between devices: 45.3 us -> 1.79 us
  matrix products: 26 us -> 0 us
  Pallas kernels: 0 us -> 9.55 us
  local copies, waits for them, and re-layouts: 3.3 us -> 0 us
    ppermute x23 -> x4, starting transfers between devices: 118 us -> 23.9 us  [permute(): lax.ppermute(value, AXES, [(i, partner(i) % members) for i in range(membe...]
    ppermute x23 -> x4, waiting for transfers between devices: 45.3 us -> 1.79 us  [permute(): lax.ppermute(value, AXES, [(i, partner(i) % members) for i in range(membe...]
    dot_general x31 -> x0, matrix products: 26 us -> none  [the longest x12 10.2 us: couple(): jnp.dot(interaction_partner, coupling[height - 1, position_index], precis...]
    pallas_call x0 -> x6, Pallas kernels: none -> 9.55 us  [the longest x1 3.7 us: local(): call(near_kernel, [((4, 32, 256), F32), ((4, 32, 64), F32), ((32, 64), F3...]
    all_to_all x0 -> x1, starting transfers between devices: none -> 5.72 us  [local(): chips = lax.all_to_all(chunk, AXES, 0, 0, axis_index_groups=groups)]
  transfers between devices with their start and end apart: 23 -> 5, of which waited for: 11 -> 1; matrix products, arithmetic and copies ran while one was open for 12% -> 0% of each run, Pallas kernels for 0% -> 15%
where the time goes in v1:
time: 41.4 us; the launch traced here: 41.1 us
  starting transfers between devices  29.6 us (71%)
  Pallas kernels  9.55 us (23%)
  waiting for transfers between devices  1.79 us (4%)
    ppermute x4, starting transfers between devices, permute(): lax.ppermute(value, AXES, [(i, partner(i) % members) for i in range(membe...  23.9 us
    all_to_all x1, starting transfers between devices, local(): chips = lax.all_to_all(chunk, AXES, 0, 0, axis_index_groups=groups)  5.72 us
    pallas_call x1, Pallas kernels, local(): call(near_kernel, [((4, 32, 256), F32), ((4, 32, 64), F32), ((32, 64), F3...  3.7 us
    ppermute x4, waiting for transfers between devices, permute(): lax.ppermute(value, AXES, [(i, partner(i) % members) for i in range(membe...  1.79 us
    pallas_call x1, Pallas kernels, local(): call(moments_kernel, [((4, 32, 256), BF16), ((4, 64, 256), BF16), ((4, 64...  1.42 us
    pallas_call x1, Pallas kernels, local(): call(levels_kernel, [((32, 128), BF16), ((32, 64), F32)], [VMEM] * 4, [pl...  1.23 us
    pallas_call x1, Pallas kernels, local(): call(product_kernel, [((4, 32, 256), F32)], [VMEM] * 6)  1.16 us
    pallas_call x1, Pallas kernels, local(): call(weights_kernel, [((3, 256, 64), BF16), ((3, 64, 128), BF16), ((3, 51...  1.15 us
  transfers between devices with their start and end apart: 5, of which 1 were waited for; matrix products, arithmetic and copies ran while one was open for 0% of the time, Pallas kernels for 15%

profile of v1, /device:TPU:1, one launch (start us, length us, event | category | flops | bytes accessed | tf_op | source)
XLA Modules:
  0.0 41.1 jit_solution(9907789493637165358)
XLA Ops:
  0.0 1.4 %shard_map.91 = (bf16[4,32,256]{2,1,0:T(8,128)(2,1)S(1)}, bf16[4,64,256]{2,1,0:T(8,128)(2,1)S(1)}, bf16[4,64,64]{2,1,0:T(8,128)(2,1)S(1)}, bf16[6,32,256]{2,1,0:T(8,128)(2,1)S(1)}) custom-call(bf16[4,32,256]{2,1,0:T(8,128)(2,1)} %x_hbm.1, bf16[4,64,256]{2,1,0:T(8,128)(2,1)} %basis_hbm.1, bf16[4,64,64]{2,1,0:T(8,128)(2,1)} %transfer_hbm.1), custom_call_target="tpu_custom_call" | custom-call | tf_op jit(solution)/shard_map/pallas_call | solution.py:236
  1.4 8.8 %collective-permute-start = (bf16[6,32,256]{2,1,0:T(8,128)(2,1)S(1)}, bf16[6,32,256]{2,1,0:T(8,128)(2,1)S(1)}, u32[]{:S(2)}, u32[]{:S(2)}) collective-permute-start(bf16[6,32,256]{2,1,0:T(8,128)(2,1)S(1)} %get-tuple-element.23.mine_ref), channel_id=1, source_target_pairs={{0,1},{1,0},{2,3},{3,2},{4,5},{5,4},{6,7},{7,6},{8,9},{9,8},{10,11... | collective-permute-start | bytes 294920 | tf_op jit(solution)/shard_map/ppermute | solution.py:221
  10.2 1.1 %shard_map.92 = (bf16[3,256,64]{2,1,0:T(8,128)(2,1)S(1)}, bf16[3,64,128]{2,1,0:T(8,128)(2,1)S(1)}, bf16[3,512,64]{2,1,0:T(8,128)(2,1)S(1)}, bf16[1024,64]{1,0:T(8,128)(2,1)S(1)}, bf16[512,64]{1,0:T(8,128)(2,1)S(1)}) custom-call(bf16[3,2,64,64]{3,2,1,0:T(8,128)(2,1)} %level_hbm.1, bf16[3,4,64,64]{3,2,1,0:T(8,128)(2,1)} %coupling_hbm.1, ...), custom_call_target="tpu_custom_call" | custom-call | bytes 2000000 | tf_op jit(solution)/shard_map/pallas_call | solution.py:243
  11.4 0.0 collective-permute-done.sibling_ref
  11.4 0.9 %shard_map.93 = (bf16[16,32,128]{2,1,0:T(8,128)(2,1)}, bf16[6,32,256]{2,1,0:T(8,128)(2,1)S(1)}, bf16[32,256]{1,0:T(8,128)(2,1)S(1)}) custom-call(bf16[4,32,256]{2,1,0:T(8,128)(2,1)S(1)} %get-tuple-element.22.x_ref, bf16[6,32,256]{2,1,0:T(8,128)(2,1)S(1)} %get-tuple-element.23.mine_ref, bf16[6,32,256]{2,1,0:T(8,128)(2,1)S(1)} %collective-permute-done.sibling_ref, ...), custom_call_target="tpu_custom_call" | custom-call | tf_op jit(solution)/shard_map/pallas_call | solution.py:262
  12.3 5.7 %all-to-all-start = ((bf16[16,32,128]{2,1,0:T(8,128)(2,1)}), bf16[16,32,128]{2,1,0:T(8,128)(2,1)S(1)}, u32[]{:S(2)}, u32[]{:S(2)}) async-start(bf16[16,32,128]{2,1,0:T(8,128)(2,1)} %get-tuple-element.27), calls=%async_computation | async-start | bytes 262144 | tf_op jit(solution)/shard_map/all_to_all | solution.py:272
  18.0 3.8 %collective-permute-start.1 = (bf16[6,32,256]{2,1,0:T(8,128)(2,1)S(1)}, bf16[6,32,256]{2,1,0:T(8,128)(2,1)S(1)}, u32[]{:S(2)}, u32[]{:S(2)}) collective-permute-start(bf16[6,32,256]{2,1,0:T(8,128)(2,1)S(1)} %get-tuple-element.25), channel_id=1, source_target_pairs={{0,511},{1,2},{2,1},{3,4},{4,3},{5,6},{6,5},{7,8},{8,7},{9,10},{10... | collective-permute-start | bytes 294920 | tf_op jit(solution)/shard_map/ppermute | solution.py:221
  21.8 9.1 %collective-permute-start.2 = (bf16[32,256]{1,0:T(8,128)(2,1)S(1)}, bf16[32,256]{1,0:T(8,128)(2,1)S(1)}, u32[]{:S(2)}, u32[]{:S(2)}) collective-permute-start(bf16[32,256]{1,0:T(8,128)(2,1)S(1)} %get-tuple-element.26), channel_id=1, source_target_pairs={{0,3},{1,510},{2,5},{3,0},{4,7},{5,2},{6,9},{7,4},{8,11},{9,6},{10... | collective-permute-start | bytes 49160 | tf_op jit(solution)/shard_map/ppermute | solution.py:221
  30.9 0.0 all-to-all-done.chips_ref
  31.0 1.2 %shard_map.94 = (bf16[32,128]{1,0:T(8,128)(2,1)S(1)}, f32[32,64]{1,0:T(8,128)S(1)}) custom-call(bf16[16,32,128]{2,1,0:T(8,128)(2,1)S(1)} %all-to-all-done.chips_ref, bf16[3,256,64]{2,1,0:T(8,128)(2,1)S(1)} %get-tuple-element.24.up_ref, bf16[3,64,128]{2,1,0:T(8,128)(2,1)S(1)} %get-tuple-element.28.down_ref, bf16[3,512,64]{2,1,0:T(8,128)(2,1)S(1)} %get-tuple-element.29.coupling_ref), custom_call_target="tpu_custom_call" | custom-call | tf_op jit(solution)/shard_map/pallas_call | solution.py:275
  32.2 2.2 %collective-permute-start.3 = (bf16[32,128]{1,0:T(8,128)(2,1)S(1)}, bf16[32,128]{1,0:T(8,128)(2,1)S(1)}, u32[]{:S(2)}, u32[]{:S(2)}) collective-permute-start(bf16[32,128]{1,0:T(8,128)(2,1)S(1)} %get-tuple-element.36), channel_id=1, source_target_pairs={{0,496},{1,497},{2,498},{3,499},{4,500},{5,501},{6,502},{7,503},{8... | collective-permute-start | bytes 24584 | tf_op jit(solution)/shard_map/ppermute | solution.py:221
  34.4 0.0 collective-permute-done.2.nodes_ref
  34.4 0.0 collective-permute-done.1.next_ref
  34.4 3.7 %shard_map.95 = (f32[4,32,256]{2,1,0:T(8,128)S(1)}, f32[4,32,64]{2,1,0:T(8,128)S(1)}, f32[32,64]{1,0:T(8,128)S(1)}) custom-call(bf16[4,32,256]{2,1,0:T(8,128)(2,1)S(1)} %get-tuple-element.22.x_ref, bf16[6,32,256]{2,1,0:T(8,128)(2,1)S(1)} %collective-permute-done.sibling_ref, bf16[6,32,256]{2,1,0:T(8,128)(2,1)S(1)} %collective-permute-done.1.next_ref, ...), custom_call_target="tpu_custom_call" | custom-call | flops 200000000 | bytes 4000000 | tf_op jit(solution)/shard_map/pallas_call | solution.py:282
  38.1 1.8 %collective-permute-done.3.given_ref = bf16[32,128]{1,0:T(8,128)(2,1)S(1)} collective-permute-done((bf16[32,128]{1,0:T(8,128)(2,1)S(1)}, bf16[32,128]{1,0:T(8,128)(2,1)S(1)}, u32[]{:S(2)}, u32[]{:S(2)}) %collective-permute-start.3) | collective-permute-done | bytes 8224 | tf_op jit(solution)/shard_map/ppermute | solution.py:221
  39.9 1.2 %shard_map.96 = f32[4,32,256]{2,1,0:T(8,128)} custom-call(f32[4,32,256]{2,1,0:T(8,128)S(1)} %get-tuple-element.33.near_ref, f32[4,32,64]{2,1,0:T(8,128)S(1)} %get-tuple-element.34.far_ref, f32[32,64]{1,0:T(8,128)S(1)} %get-tuple-element.35.field_ref, bf16[32,128]{1,0:T(8,128)(2,1)S(1)} %collective-permute-done.3.given_ref, ...), custom_call_target="tpu_custom_call" | custom-call | tf_op jit(solution)/shard_map/pallas_call | solution.py:295
Async XLA Ops:
  1.4 10.0 %collective-permute-start = (bf16[6,32,256]{2,1,0:T(8,128)(2,1)S(1)}, bf16[6,32,256]{2,1,0:T(8,128)(2,1)S(1)}, u32[]{:S(2)}, u32[]{:S(2)}) collective-permute-start(bf16[6,32,256]{2,1,0:T(8,128)(2,1)S(1)} %get-tuple-element.23.mine_ref), channel_id=1, source_target_pairs={{0,1},{1,0},{2,3},{3,2},{4,5},{5,4},{6,7},{7,6},{8,9},{9,8},{10,11... | collective-permute-start | bytes 294920 | tf_op jit(solution)/shard_map/ppermute | solution.py:221
  12.3 18.7 %all-to-all-start = ((bf16[16,32,128]{2,1,0:T(8,128)(2,1)}), bf16[16,32,128]{2,1,0:T(8,128)(2,1)S(1)}, u32[]{:S(2)}, u32[]{:S(2)}) async-start(bf16[16,32,128]{2,1,0:T(8,128)(2,1)} %get-tuple-element.27), calls=%async_computation | async-start | bytes 262144 | tf_op jit(solution)/shard_map/all_to_all | solution.py:272
  18.0 16.4 %collective-permute-start.1 = (bf16[6,32,256]{2,1,0:T(8,128)(2,1)S(1)}, bf16[6,32,256]{2,1,0:T(8,128)(2,1)S(1)}, u32[]{:S(2)}, u32[]{:S(2)}) collective-permute-start(bf16[6,32,256]{2,1,0:T(8,128)(2,1)S(1)} %get-tuple-element.25), channel_id=1, source_target_pairs={{0,511},{1,2},{2,1},{3,4},{4,3},{5,6},{6,5},{7,8},{8,7},{9,10},{10... | collective-permute-start | bytes 294920 | tf_op jit(solution)/shard_map/ppermute | solution.py:221
  21.8 12.6 %collective-permute-start.2 = (bf16[32,256]{1,0:T(8,128)(2,1)S(1)}, bf16[32,256]{1,0:T(8,128)(2,1)S(1)}, u32[]{:S(2)}, u32[]{:S(2)}) collective-permute-start(bf16[32,256]{1,0:T(8,128)(2,1)S(1)} %get-tuple-element.26), channel_id=1, source_target_pairs={{0,3},{1,510},{2,5},{3,0},{4,7},{5,2},{6,9},{7,4},{8,11},{9,6},{10... | collective-permute-start | bytes 49160 | tf_op jit(solution)/shard_map/ppermute | solution.py:221
  32.2 7.7 %collective-permute-start.3 = (bf16[32,128]{1,0:T(8,128)(2,1)S(1)}, bf16[32,128]{1,0:T(8,128)(2,1)S(1)}, u32[]{:S(2)}, u32[]{:S(2)}) collective-permute-start(bf16[32,128]{1,0:T(8,128)(2,1)S(1)} %get-tuple-element.36), channel_id=1, source_target_pairs={{0,496},{1,497},{2,498},{3,499},{4,500},{5,501},{6,502},{7,503},{8... | collective-permute-start | bytes 24584 | tf_op jit(solution)/shard_map/ppermute | solution.py:221

commit v2 on v1

--- a/solution.py
+++ b/solution.py
@@ -9,6 +9,7 @@
 NREACH = 3
 OFFSETS = (-3, -2, 2, 3)
 CHIPS = 8
+EARLY = 6
 BF16, F32 = jnp.bfloat16, jnp.float32
 VMEM = pl.BlockSpec(memory_space=pltpu.VMEM)
 HBM = pl.BlockSpec(memory_space=pltpu.HBM)
@@ -82,7 +83,7 @@
     node_ref[...] = stacked([node[0, k] for k in range(4)], 0)
 
 
-def pair_kernel(x_ref, mine_ref, sibling_ref, up_ref, chunk_ref, next_ref, nodes_ref):
+def pair_kernel(x_ref, mine_ref, sibling_ref, up_ref, chunk_ref, next_ref, pairs_ref):
     odd = lax.axis_index("near") % 2
     mine = mine_ref[5][:, :128]
     sibling = sibling_ref[5][:, :128]
@@ -91,17 +92,17 @@
     chip = halves(dot(jnp.concatenate([even_node, odd_node], axis=1), up_ref[0]))
     for j in range(chunk_ref.shape[0]):
         chunk_ref[j] = chip
-    nodes_ref[...] = jnp.concatenate([mine, sibling], axis=1)
     next_ref[0:3] = x_ref[pl.ds(odd, 3)]
     next_ref[3:5] = mine_ref[3:5]
-    next_ref[5] = jnp.concatenate([sibling, sibling], axis=1)
+    next_ref[5] = jnp.concatenate([mine, sibling], axis=1)
+    pairs_ref[...] = jnp.concatenate([mine, sibling], axis=1)
 
 
 def levels_kernel(
     chips_ref, up_ref, down_ref, coupling_ref, send_ref, own_ref, quads, octets
 ):
     near = lax.axis_index("near")
-    side = lax.axis_index("leaf") % 2
+    side = (lax.axis_index("leaf") + 1) % 2
     z = near // 2
     rows = [jnp.concatenate([chips_ref[2 * q], chips_ref[2 * q + 1]], axis=1) for q in range(8)]
     second = halves(dot(jnp.concatenate(rows, axis=0), up_ref[1])).reshape(8, 32, 128)
@@ -139,22 +140,87 @@
     send_ref[...] = halves(field[32:])
 
 
-def near_kernel(
-    x_ref, sibling_ref, next_ref, nodes_ref, own_ref, leaf_ref, node_ref, cols_hbm, blocks_hbm,
-    near_ref, far_ref, field_ref, window, cols, blocks, semaphores,
-):
-    copies = load(
+def near_all(window, cols, blocks, copies, near_ref, first):
+    copies[4].wait()
+    for j in range(4):
+        total = None
+        copies[j].wait()
+        for k in range(7):
+            place = (cols[j, k] - first) & 2047
+            term = dot_nt(window[place], blocks[j, k])
+            total = term if total is None else total + term
+        near_ref[j] = total
+
+
+def load_near(cols_hbm, blocks_hbm, cols, blocks, semaphores):
+    return load(
         [blocks_hbm.at[j] for j in range(4)] + [cols_hbm],
         [blocks.at[j] for j in range(4)] + [cols],
         semaphores,
     )
+
+
+def position():
     near = lax.axis_index("near")
-    odd = near % 2
     first = (lax.axis_index("leaf") * (2 * CHIPS) + near) * 4 - NREACH
-    is_odd = odd == 1
-    window[3:7] = x_ref[...]
-    window[0:3] = jnp.where(is_odd, sibling_ref[0:3], next_ref[0:3])
-    window[7:10] = jnp.where(is_odd, next_ref[0:3], sibling_ref[0:3])
+    return near % 2 == 1, near < EARLY, first
+
+
+def early_kernel(
+    x_ref, sibling_ref, cols_hbm, blocks_hbm, near_ref, window, cols, blocks, semaphores
+):
+    is_odd, early, first = position()
+
+    @pl.when(early)
+    def _():
+        copies = load_near(cols_hbm, blocks_hbm, cols, blocks, semaphores)
+        window[3:7] = x_ref[...]
+        halo = sibling_ref[0:3]
+        none = jnp.zeros_like(halo)
+        window[0:3] = jnp.where(is_odd, halo, none)
+        window[7:10] = jnp.where(is_odd, none, halo)
+        near_all(window, cols, blocks, copies, near_ref, first)
+
+
+def near_kernel(
+    x_ref, sibling_ref, next_ref, leaf_ref, begun_ref, cols_hbm, blocks_hbm,
+    near_ref, far_ref, window, cols, blocks, semaphores,
+):
+    is_odd, early, first = position()
+
+    @pl.when(early)
+    def _():
+        copy = pltpu.make_async_copy(cols_hbm, cols, semaphores.at[4])
+        copy.start()
+        near_ref[...] = begun_ref[...]
+        copy.wait()
+        rest = [(j, t) for j in range(3) for t in range(j, 3)]
+        leaves = [jnp.where(is_odd, 3 - j, j) for j in range(3)]
+        copies = []
+        for slot, (j, t) in enumerate(rest):
+            place = jnp.where(is_odd, 9 - t, t)
+            k = sum(
+                jnp.where(((cols[leaves[j], i] - first) & 2047) == place, i, 0) for i in range(7)
+            )
+            copies.append(
+                pltpu.make_async_copy(
+                    blocks_hbm.at[leaves[j], k], blocks.at[0, slot], semaphores.at[slot]
+                )
+            )
+            copies[-1].start()
+        for slot, (j, t) in enumerate(rest):
+            copies[slot].wait()
+            place = jnp.where(is_odd, 2 - t, t)
+            near_ref[leaves[j]] += dot_nt(next_ref[place], blocks[0, slot])
+
+    @pl.when(jnp.logical_not(early))
+    def _():
+        copies = load_near(cols_hbm, blocks_hbm, cols, blocks, semaphores)
+        window[3:7] = x_ref[...]
+        window[0:3] = jnp.where(is_odd, sibling_ref[0:3], next_ref[0:3])
+        window[7:10] = jnp.where(is_odd, next_ref[0:3], sibling_ref[0:3])
+        near_all(window, cols, blocks, copies, near_ref, first)
+
     zero = jnp.zeros((32, 128), BF16)
     left, right = [], []
     for pair in (3, 4):
@@ -171,30 +237,25 @@
     coupled = dot(jnp.concatenate(rows, axis=0), leaf_ref[...])
     for j in range(4):
         far_ref[j] = coupled[32 * j : 32 * j + 32]
-    direct = nodes_ref[:, :128]
-    beside = nodes_ref[:, 128:]
-    adjacent = next_ref[5][:, :128]
+
+
+def product_kernel(
+    near_ref, far_ref, own_ref, given_ref, next_ref, facing_ref, node_ref, transfer_ref, basis_ref,
+    out_ref,
+):
+    is_odd = lax.axis_index("near") % 2 == 1
+    zero = jnp.zeros((32, 128), BF16)
+    adjacent = next_ref[5][:, 128:]
+    distant, close = facing_ref[:, :128], facing_ref[:, 128:]
     row = [
-        jnp.where(is_odd, direct, zero),
-        jnp.where(is_odd, beside, adjacent),
-        jnp.where(is_odd, adjacent, beside),
-        jnp.where(is_odd, zero, direct),
+        jnp.where(is_odd, distant, zero),
+        jnp.where(is_odd, close, adjacent),
+        jnp.where(is_odd, adjacent, close),
+        jnp.where(is_odd, zero, distant),
     ]
-    field_ref[...] = own_ref[...] + dot(jnp.concatenate(row, axis=1), node_ref[...])
-    copies[4].wait()
-    for j in range(4):
-        total = None
-        copies[j].wait()
-        for k in range(7):
-            place = (cols[j, k] - first) & 2047
-            term = dot_nt(window[place], blocks[j, k])
-            total = term if total is None else total + term
-        near_ref[j] = total
-
-
-def product_kernel(near_ref, far_ref, field_ref, given_ref, transfer_ref, basis_ref, out_ref):
     given = given_ref[...].astype(F32)
-    field = halves(field_ref[...] + given[:, :64] + given[:, 64:])
+    field = own_ref[...] + dot(jnp.concatenate(row, axis=1), node_ref[...])
+    field = halves(field + given[:, :64] + given[:, 64:])
     for j in range(4):
         leaf_field = dot_nt(field, stacked([transfer_ref[j]], 1)) + far_ref[j]
         out_ref[j] = dot(halves(leaf_field), stacked([basis_ref[j]], 0)) + near_ref[j]
@@ -259,41 +320,54 @@
         ],
         size=2_000_000,
     )(*in_hbm(level_transfer, level_coupling, leaf_coupling, node_coupling))
-    chunk, package, nodes = call(
+    chunk, package, pairs = call(
         pair_kernel,
         [((16, 32, 128), BF16), ((6, 32, 256), BF16), ((32, 256), BF16)],
         [VMEM] * 4,
     )(x, package, sibling, up)
+    (begun,) = call(
+        early_kernel,
+        [((4, 32, 256), F32)],
+        [VMEM] * 2 + [HBM] * 2,
+        [
+            pltpu.VMEM((10, 32, 256), BF16),
+            pltpu.SMEM((4, 7), jnp.int32),
+            pltpu.VMEM((4, 7, 256, 256), BF16),
+            pltpu.SemaphoreType.DMA((5,)),
+        ],
+    )(x, sibling, *in_hbm(near_cols, near_blocks))
+    chunk, begun = lax.optimization_barrier((chunk, begun))
     groups = [
-        [2 * block * pair + block * side + 2 * z + core for side in range(2) for z in range(CHIPS)]
+        [(2 * block * pair + block * (side - 1) + 2 * z + core) % 512 for side in range(2) for z in range(CHIPS)]
         for pair in range(lax.axis_size("leaf") // 2)
         for core in range(2)
     ]
     chips = lax.all_to_all(chunk, AXES, 0, 0, axis_index_groups=groups)
     after = permute(package, lambda i: i + 1 if i % 2 else i - 1)
-    nodes = permute(nodes, lambda i: i - 3 if i % 2 else i + 3)
+    facing = permute(pairs, lambda i: i - 3 if i % 2 else i + 3)
     send, own = call(
         levels_kernel,
         [((32, 128), BF16), ((32, 64), F32)],
         [VMEM] * 4,
         [pltpu.VMEM((8, 32, 128), BF16), pltpu.VMEM((4, 32, 128), BF16)],
     )(chips, up, down, coupling)
-    given = permute(send, lambda i: i + block if i // block % 2 else i - block)
-    near, far, field = call(
+    given = permute(send, lambda i: i - block if i // block % 2 else i + block)
+
+    near, far = call(
         near_kernel,
-        [((4, 32, 256), F32), ((4, 32, 64), F32), ((32, 64), F32)],
-        [VMEM] * 7 + [HBM] * 2,
+        [((4, 32, 256), F32), ((4, 32, 64), F32)],
+        [VMEM] * 5 + [HBM] * 2,
         [
             pltpu.VMEM((10, 32, 256), BF16),
             pltpu.SMEM((4, 7), jnp.int32),
             pltpu.VMEM((4, 7, 256, 256), BF16),
-            pltpu.SemaphoreType.DMA((5,)),
+            pltpu.SemaphoreType.DMA((6,)),
         ],
         flops=200_000_000,
         size=4_000_000,
-    )(x, sibling, after, nodes, own, leaf, node, *in_hbm(near_cols, near_blocks))
-    (out,) = call(product_kernel, [((4, 32, 256), F32)], [VMEM] * 6)(
-        near, far, field, given, transfer, basis
+    )(x, sibling, after, leaf, begun, *in_hbm(near_cols, near_blocks))
+    (out,) = call(product_kernel, [((4, 32, 256), F32)], [VMEM] * 9)(
+        near, far, own, given, after, facing, node, transfer, basis
     )
     return out
 

time: 41.4 us -> 38.8 us (0.937)
  starting transfers between devices: 29.6 us -> 26.1 us
  Pallas kernels: 9.55 us -> 12.2 us
  waiting for transfers between devices: 1.79 us -> 0.01 us
    ppermute x4, starting transfers between devices: 23.9 us -> 19.5 us  [permute(): lax.ppermute(value, AXES, [(i, partner(i) % members) for i in range(membe...]
    pallas_call x2 -> x3, Pallas kernels: 4.86 us -> 7.51 us  [the longest x1 3.59 us: local(): call(early_kernel, [((4, 32, 256), F32)], [VMEM] * 2 + [HBM] * 2, [pltpu....]
    ppermute x4, waiting for transfers between devices: 1.79 us -> 0.01 us  [permute(): lax.ppermute(value, AXES, [(i, partner(i) % members) for i in range(membe...]
    all_to_all x1, starting transfers between devices: 5.72 us -> 6.56 us  [local(): chips = lax.all_to_all(chunk, AXES, 0, 0, axis_index_groups=groups)]
  transfers between devices with their start and end apart: 5 -> 5, of which waited for: 1 -> 0; matrix products, arithmetic and copies ran while one was open for 0% -> 0% of each run, Pallas kernels for 15% -> 13%
where the time goes in v2:
time: 38.8 us; the launch traced here: 38.4 us
  starting transfers between devices  26.1 us (67%)
  Pallas kernels  12.2 us (31%)
    ppermute x4, starting transfers between devices, permute(): lax.ppermute(value, AXES, [(i, partner(i) % members) for i in range(membe...  19.5 us
    all_to_all x1, starting transfers between devices, local(): chips = lax.all_to_all(chunk, AXES, 0, 0, axis_index_groups=groups)  6.56 us
    pallas_call x1, Pallas kernels, local(): call(early_kernel, [((4, 32, 256), F32)], [VMEM] * 2 + [HBM] * 2, [pltpu....  3.59 us
    pallas_call x1, Pallas kernels, local(): call(near_kernel, [((4, 32, 256), F32), ((4, 32, 64), F32)], [VMEM] * 5 +...  2.69 us
    pallas_call x1, Pallas kernels, local(): call(moments_kernel, [((4, 32, 256), BF16), ((4, 64, 256), BF16), ((4, 64...  1.42 us
    pallas_call x1, Pallas kernels, local(): call(levels_kernel, [((32, 128), BF16), ((32, 64), F32)], [VMEM] * 4, [pl...  1.24 us
    pallas_call x1, Pallas kernels, local(): call(product_kernel, [((4, 32, 256), F32)], [VMEM] * 9)  1.23 us
    pallas_call x1, Pallas kernels, local(): call(weights_kernel, [((3, 256, 64), BF16), ((3, 64, 128), BF16), ((3, 51...  1.15 us
  transfers between devices with their start and end apart: 5, of which 0 were waited for; matrix products, arithmetic and copies ran while one was open for 0% of the time, Pallas kernels for 13%

profile of v2, /device:TPU:1, one launch (start us, length us, event | category | flops | bytes accessed | tf_op | source)
XLA Modules:
  0.0 38.4 jit_solution(7366648833471118498)
XLA Ops:
  0.0 1.4 %shard_map.91 = (bf16[4,32,256]{2,1,0:T(8,128)(2,1)S(1)}, bf16[4,64,256]{2,1,0:T(8,128)(2,1)S(1)}, bf16[4,64,64]{2,1,0:T(8,128)(2,1)S(1)}, bf16[6,32,256]{2,1,0:T(8,128)(2,1)S(1)}) custom-call(bf16[4,32,256]{2,1,0:T(8,128)(2,1)} %x_hbm.1, bf16[4,64,256]{2,1,0:T(8,128)(2,1)} %basis_hbm.1, bf16[4,64,64]{2,1,0:T(8,128)(2,1)} %transfer_hbm.1), custom_call_target="tpu_custom_call" | custom-call | tf_op jit(solution)/shard_map/pallas_call | solution.py:297
  1.4 8.8 %collective-permute-start = (bf16[6,32,256]{2,1,0:T(8,128)(2,1)S(1)}, bf16[6,32,256]{2,1,0:T(8,128)(2,1)S(1)}, u32[]{:S(2)}, u32[]{:S(2)}) collective-permute-start(bf16[6,32,256]{2,1,0:T(8,128)(2,1)S(1)} %get-tuple-element.24.mine_ref), channel_id=1, source_target_pairs={{0,1},{1,0},{2,3},{3,2},{4,5},{5,4},{6,7},{7,6},{8,9},{9,8},{10,11... | collective-permute-start | bytes 294920 | tf_op jit(solution)/shard_map/ppermute | solution.py:282
  10.2 1.1 %shard_map.92 = (bf16[3,256,64]{2,1,0:T(8,128)(2,1)S(1)}, bf16[3,64,128]{2,1,0:T(8,128)(2,1)S(1)}, bf16[3,512,64]{2,1,0:T(8,128)(2,1)S(1)}, bf16[1024,64]{1,0:T(8,128)(2,1)S(1)}, bf16[512,64]{1,0:T(8,128)(2,1)S(1)}) custom-call(bf16[3,2,64,64]{3,2,1,0:T(8,128)(2,1)} %level_hbm.1, bf16[3,4,64,64]{3,2,1,0:T(8,128)(2,1)} %coupling_hbm.1, ...), custom_call_target="tpu_custom_call" | custom-call | bytes 2000000 | tf_op jit(solution)/shard_map/pallas_call | solution.py:304
  11.4 0.0 collective-permute-done.sibling_ref
  11.4 0.9 %shard_map.93 = (bf16[16,32,128]{2,1,0:T(8,128)(2,1)}, bf16[6,32,256]{2,1,0:T(8,128)(2,1)S(1)}, bf16[32,256]{1,0:T(8,128)(2,1)S(1)}) custom-call(bf16[4,32,256]{2,1,0:T(8,128)(2,1)S(1)} %get-tuple-element.23.x_ref, bf16[6,32,256]{2,1,0:T(8,128)(2,1)S(1)} %get-tuple-element.24.mine_ref, bf16[6,32,256]{2,1,0:T(8,128)(2,1)S(1)} %collective-permute-done.sibling_ref, ...), custom_call_target="tpu_custom_call" | custom-call | tf_op jit(solution)/shard_map/pallas_call | solution.py:323
  12.3 3.6 %shard_map.94.begun_ref = f32[4,32,256]{2,1,0:T(8,128)S(1)} custom-call(bf16[4,32,256]{2,1,0:T(8,128)(2,1)S(1)} %get-tuple-element.23.x_ref, bf16[6,32,256]{2,1,0:T(8,128)(2,1)S(1)} %collective-permute-done.sibling_ref, s32[4,7]{1,0:T(4,128)} %cols_hbm.3, bf16[4,7,256,256]{3,2,1,0:T(8,128)(2,1)} %blocks_hbm.3), custom_call_target="tpu_custom_call" | custom-call | tf_op jit(solution)/shard_map/pallas_call | solution.py:328
  15.9 6.6 %all-to-all-start = ((bf16[16,32,128]{2,1,0:T(8,128)(2,1)}), bf16[16,32,128]{2,1,0:T(8,128)(2,1)S(1)}, u32[]{:S(2)}, u32[]{:S(2)}) async-start(bf16[16,32,128]{2,1,0:T(8,128)(2,1)} %get-tuple-element.32), calls=%async_computation | async-start | bytes 262144 | tf_op jit(solution)/shard_map/all_to_all | solution.py:345
  22.4 3.6 %collective-permute-start.1 = (bf16[6,32,256]{2,1,0:T(8,128)(2,1)S(1)}, bf16[6,32,256]{2,1,0:T(8,128)(2,1)S(1)}, u32[]{:S(2)}, u32[]{:S(2)}) collective-permute-start(bf16[6,32,256]{2,1,0:T(8,128)(2,1)S(1)} %get-tuple-element.26), channel_id=1, source_target_pairs={{0,511},{1,2},{2,1},{3,4},{4,3},{5,6},{6,5},{7,8},{8,7},{9,10},{10... | collective-permute-start | bytes 294920 | tf_op jit(solution)/shard_map/ppermute | solution.py:282
  26.0 4.1 %collective-permute-start.3 = (bf16[32,256]{1,0:T(8,128)(2,1)S(1)}, bf16[32,256]{1,0:T(8,128)(2,1)S(1)}, u32[]{:S(2)}, u32[]{:S(2)}) collective-permute-start(bf16[32,256]{1,0:T(8,128)(2,1)S(1)} %get-tuple-element.37), channel_id=1, source_target_pairs={{0,3},{1,510},{2,5},{3,0},{4,7},{5,2},{6,9},{7,4},{8,11},{9,6},{10... | collective-permute-start | bytes 49160 | tf_op jit(solution)/shard_map/ppermute | solution.py:282
  30.1 0.0 all-to-all-done.chips_ref
  30.1 1.2 %shard_map.96 = (bf16[32,128]{1,0:T(8,128)(2,1)S(1)}, f32[32,64]{1,0:T(8,128)S(1)}) custom-call(bf16[16,32,128]{2,1,0:T(8,128)(2,1)S(1)} %all-to-all-done.chips_ref, bf16[3,256,64]{2,1,0:T(8,128)(2,1)S(1)} %get-tuple-element.25.up_ref, bf16[3,64,128]{2,1,0:T(8,128)(2,1)S(1)} %get-tuple-element.33.down_ref, bf16[3,512,64]{2,1,0:T(8,128)(2,1)S(1)} %get-tuple-element.34.coupling_ref), custom_call_target="tpu_custom_call" | custom-call | tf_op jit(solution)/shard_map/pallas_call | solution.py:348
  31.4 3.1 %collective-permute-start.2 = (bf16[32,128]{1,0:T(8,128)(2,1)S(1)}, bf16[32,128]{1,0:T(8,128)(2,1)S(1)}, u32[]{:S(2)}, u32[]{:S(2)}) collective-permute-start(bf16[32,128]{1,0:T(8,128)(2,1)S(1)} %get-tuple-element.36), channel_id=1, source_target_pairs={{0,16},{1,17},{2,18},{3,19},{4,20},{5,21},{6,22},{7,23},{8,24},{9,... | collective-permute-start | bytes 24584 | tf_op jit(solution)/shard_map/ppermute | solution.py:282
  34.5 0.0 collective-permute-done.1.next_ref
  34.5 2.7 %shard_map.95 = (f32[4,32,256]{2,1,0:T(8,128)S(1)}, f32[4,32,64]{2,1,0:T(8,128)S(1)}) custom-call(bf16[4,32,256]{2,1,0:T(8,128)(2,1)S(1)} %get-tuple-element.23.x_ref, bf16[6,32,256]{2,1,0:T(8,128)(2,1)S(1)} %collective-permute-done.sibling_ref, bf16[6,32,256]{2,1,0:T(8,128)(2,1)S(1)} %collective-permute-done.1.next_ref, ...), custom_call_target="tpu_custom_call" | custom-call | flops 200000000 | bytes 4000000 | tf_op jit(solution)/shard_map/pallas_call | solution.py:356
  37.2 0.0 collective-permute-done.3.facing_ref
  37.2 0.0 collective-permute-done.2.given_ref
  37.2 1.2 %shard_map.97 = f32[4,32,256]{2,1,0:T(8,128)} custom-call(f32[4,32,256]{2,1,0:T(8,128)S(1)} %get-tuple-element.30.near_ref, f32[4,32,64]{2,1,0:T(8,128)S(1)} %get-tuple-element.31.far_ref, f32[32,64]{1,0:T(8,128)S(1)} %get-tuple-element.35.own_ref, bf16[32,128]{1,0:T(8,128)(2,1)S(1)} %collective-permute-done.2.given_ref, ...), custom_call_target="tpu_custom_call" | custom-call | tf_op jit(solution)/shard_map/pallas_call | solution.py:369
Async XLA Ops:
  1.4 10.0 %collective-permute-start = (bf16[6,32,256]{2,1,0:T(8,128)(2,1)S(1)}, bf16[6,32,256]{2,1,0:T(8,128)(2,1)S(1)}, u32[]{:S(2)}, u32[]{:S(2)}) collective-permute-start(bf16[6,32,256]{2,1,0:T(8,128)(2,1)S(1)} %get-tuple-element.24.mine_ref), channel_id=1, source_target_pairs={{0,1},{1,0},{2,3},{3,2},{4,5},{5,4},{6,7},{7,6},{8,9},{9,8},{10,11... | collective-permute-start | bytes 294920 | tf_op jit(solution)/shard_map/ppermute | solution.py:282
  15.9 14.2 %all-to-all-start = ((bf16[16,32,128]{2,1,0:T(8,128)(2,1)}), bf16[16,32,128]{2,1,0:T(8,128)(2,1)S(1)}, u32[]{:S(2)}, u32[]{:S(2)}) async-start(bf16[16,32,128]{2,1,0:T(8,128)(2,1)} %get-tuple-element.32), calls=%async_computation | async-start | bytes 262144 | tf_op jit(solution)/shard_map/all_to_all | solution.py:345
  22.4 12.0 %collective-permute-start.1 = (bf16[6,32,256]{2,1,0:T(8,128)(2,1)S(1)}, bf16[6,32,256]{2,1,0:T(8,128)(2,1)S(1)}, u32[]{:S(2)}, u32[]{:S(2)}) collective-permute-start(bf16[6,32,256]{2,1,0:T(8,128)(2,1)S(1)} %get-tuple-element.26), channel_id=1, source_target_pairs={{0,511},{1,2},{2,1},{3,4},{4,3},{5,6},{6,5},{7,8},{8,7},{9,10},{10... | collective-permute-start | bytes 294920 | tf_op jit(solution)/shard_map/ppermute | solution.py:282
  26.0 11.1 %collective-permute-start.3 = (bf16[32,256]{1,0:T(8,128)(2,1)S(1)}, bf16[32,256]{1,0:T(8,128)(2,1)S(1)}, u32[]{:S(2)}, u32[]{:S(2)}) collective-permute-start(bf16[32,256]{1,0:T(8,128)(2,1)S(1)} %get-tuple-element.37), channel_id=1, source_target_pairs={{0,3},{1,510},{2,5},{3,0},{4,7},{5,2},{6,9},{7,4},{8,11},{9,6},{10... | collective-permute-start | bytes 49160 | tf_op jit(solution)/shard_map/ppermute | solution.py:282
  31.4 5.8 %collective-permute-start.2 = (bf16[32,128]{1,0:T(8,128)(2,1)S(1)}, bf16[32,128]{1,0:T(8,128)(2,1)S(1)}, u32[]{:S(2)}, u32[]{:S(2)}) collective-permute-start(bf16[32,128]{1,0:T(8,128)(2,1)S(1)} %get-tuple-element.36), channel_id=1, source_target_pairs={{0,16},{1,17},{2,18},{3,19},{4,20},{5,21},{6,22},{7,23},{8,24},{9,... | collective-permute-start | bytes 24584 | tf_op jit(solution)/shard_map/ppermute | solution.py:282

commit v3 on v1

v3 whole, which is shorter than its diff:
```python
import jax
import jax.numpy as jnp
from jax import lax
from jax.experimental import pallas as pl
from jax.experimental.pallas import tpu as pltpu
from jax.sharding import PartitionSpec as P

AXES = ("leaf", "near")
NREACH = 3
OFFSETS = (-3, -2, 2, 3)
CHIPS = 8
EARLY = 6
BF16, F32 = jnp.bfloat16, jnp.float32
VMEM = pl.BlockSpec(memory_space=pltpu.VMEM)
HBM = pl.BlockSpec(memory_space=pltpu.HBM)


def dot(a, b):
    return lax.dot_general(a, b, (((1,), (0,)), ((), ())), preferred_element_type=F32)


def dot_nt(a, b):
    return lax.dot_general(a, b, (((1,), (1,)), ((), ())), preferred_element_type=F32)


def halves(value):
    high = value.astype(BF16)
    low = (value - high.astype(F32)).astype(BF16)
    return jnp.concatenate([high, low], axis=1)


def stacked(weights, axis):
    return jnp.concatenate([w for w in weights for _ in range(2)], axis=axis)


def load(sources, targets, semaphores):
    copies = [
        pltpu.make_async_copy(source, target, semaphores.at[i])
        for i, (source, target) in enumerate(zip(sources, targets, strict=True))
    ]
    for copy in copies:
        copy.start()
    return copies


def moments_kernel(
    x_hbm, basis_hbm, transfer_hbm, level_hbm, coupling_hbm, leaf_hbm, node_hbm,
    x_ref, basis_ref, transfer_ref, chunk_ref, sibling_ref, next_ref, level_ref, coupling_ref,
    leaf_ref, node_ref, semaphores,
):
    odd = lax.axis_index("near") % 2
    copies = load(
        (x_hbm, basis_hbm, transfer_hbm, level_hbm, coupling_hbm, node_hbm, leaf_hbm),
        (x_ref, basis_ref, transfer_ref, level_ref, coupling_ref, node_ref, leaf_ref),
        semaphores,
    )
    copies[0].wait()
    copies[1].wait()
    parts = [halves(dot_nt(x_ref[j], basis_ref[j])) for j in range(4)]
    copies[2].wait()
    weights = stacked([transfer_ref[j] for j in range(4)], 0)
    moments = halves(dot(jnp.concatenate(parts, axis=1), weights))
    for j in range(chunk_ref.shape[0]):
        chunk_ref[j] = moments
    for ref, first in ((sibling_ref, 1 - odd), (next_ref, odd)):
        ref[0:3] = x_ref[pl.ds(first, 3)]
        ref[3] = jnp.concatenate(parts[:2], axis=1)
        ref[4] = jnp.concatenate(parts[2:], axis=1)
    for copy in copies[3:]:
        copy.wait()


def levels_kernel(
    nodes_ref, level_ref, coupling_ref, node_ref, even_ref, odd_ref, own_ref,
    chips, quads, octets,
):
    near = lax.axis_index("near")
    is_odd = lax.axis_index("leaf") % 2 == 1
    below = nodes_ref
    for c, table in ((0, chips), (1, quads), (2, octets)):
        count = table.shape[0]
        rows = [jnp.concatenate([below[2 * i], below[2 * i + 1]], axis=1) for i in range(count)]
        moments = halves(dot(jnp.concatenate(rows, axis=0), stacked([level_ref[c, 0], level_ref[c, 1]], 0)))
        table[...] = moments.reshape(count, 32, 128)
        below = table

    def partners(table, target, height):
        count = table.shape[0]
        node = target >> height
        parity = (near >> height) % 2
        blocks = []
        for k, offset in enumerate(OFFSETS):
            partner = node + offset
            valid = (partner >= 0) & (partner < count)
            if k == 0:
                valid = valid & (parity == 1)
            if k == 3:
                valid = valid & (parity == 0)
            block = table[jnp.clip(partner, 0, count - 1)]
            blocks.append(jnp.where(valid, block, jnp.zeros_like(block)))
        return blocks

    size = 2 * CHIPS
    targets = (near, near - size, near + size)
    rows = [
        jnp.concatenate(
            [
                block
                for c, table in ((1, chips), (2, quads), (3, octets))
                for block in partners(table, target, c)
            ],
            axis=1,
        )
        for target in targets
    ]
    down, tables = None, []
    for c in range(3):
        chosen = level_ref[c, (near >> c) % 2]
        if c == 0:
            down = chosen
        else:
            down = halves(dot(down, chosen if c == 1 else stacked([chosen], 0)))
        matrices = jnp.concatenate([coupling_ref[c, k] for k in range(4)], axis=0)
        if c == 0:
            tables.append(dot_nt(matrices, down))
        else:
            tables.append(dot_nt(jnp.concatenate([matrices, matrices], axis=1), down))
    table = halves(jnp.concatenate(tables, axis=0))
    table = stacked([table[64 * i : 64 * i + 64] for i in range(12)], 0)
    both = dot(jnp.concatenate(rows, axis=0), table)
    field = both[:, :64] + both[:, 64:]
    beside = jnp.concatenate(partners(nodes_ref, near, 0), axis=1)
    own_ref[...] = field[:32] + dot(beside, stacked([node_ref[0, k] for k in range(4)], 0))
    before = [halves(field[32:64])] + partners(nodes_ref, near - size, 0)[2:]
    after = [halves(field[64:])] + partners(nodes_ref, near + size, 0)[:2]
    for i in range(3):
        even_ref[i] = jnp.where(is_odd, before[i], after[i])
        odd_ref[i] = jnp.where(is_odd, after[i], before[i])


def near_all(window, cols, blocks, copies, near_ref, first):
    copies[4].wait()
    for j in range(4):
        total = None
        copies[j].wait()
        for k in range(7):
            place = (cols[j, k] - first) & 2047
            term = dot_nt(window[place], blocks[j, k])
            total = term if total is None else total + term
        near_ref[j] = total


def load_near(cols_hbm, blocks_hbm, cols, blocks, semaphores):
    return load(
        [blocks_hbm.at[j] for j in range(4)] + [cols_hbm],
        [blocks.at[j] for j in range(4)] + [cols],
        semaphores,
    )


def position():
    near = lax.axis_index("near")
    first = (lax.axis_index("leaf") * (2 * CHIPS) + near) * 4 - NREACH
    early = (near < EARLY) & (first + NREACH > 0)
    return near % 2 == 1, early, first


MISSING = [(j, t) for j in range(3) for t in range(j, 3)]
MISSING += [(3 - j, 9 - t) for j, t in MISSING]


def fourths(value):
    high = value.astype(BF16)
    low = (value - high.astype(F32)).astype(BF16)
    rows = [jnp.concatenate([high, high], axis=1), jnp.concatenate([low, jnp.zeros_like(low)], axis=1)]
    return jnp.concatenate(rows, axis=0)


def expand(transfer_ref, basis_ref, table_ref):
    for j in range(4):
        product = lax.dot_general(
            transfer_ref[j], basis_ref[j], (((0,), (0,)), ((), ())), preferred_element_type=F32
        )
        high = product.astype(BF16)
        columns = slice(256 * j, 256 * j + 256)
        table_ref[0:64, columns] = high
        table_ref[64:128, columns] = (product - high.astype(F32)).astype(BF16)


def early_kernel(
    x_ref, transfer_ref, basis_ref, cols_hbm, blocks_hbm,
    near_ref, rest_ref, table_ref, window, cols, blocks, semaphores,
):
    _, early, first = position()

    @pl.when(early)
    def _():
        copies = load_near(cols_hbm, blocks_hbm, cols, blocks, semaphores)
        expand(transfer_ref, basis_ref, table_ref)
        window[3:7] = x_ref[...]
        none = jnp.zeros((3, 32, 256), BF16)
        window[0:3] = none
        window[7:10] = none
        near_all(window, cols, blocks, copies, near_ref, first)
        for slot, (j, t) in enumerate(MISSING):
            k = sum(jnp.where(((cols[j, i] - first) & 2047) == t, i, 0) for i in range(7))
            rest_ref[slot] = blocks[j, k]


def near_kernel(
    x_ref, sibling_ref, next_ref, own_ref, leaf_ref, transfer_ref, basis_ref,
    begun_ref, rest_ref, early_table_ref, cols_hbm, blocks_hbm,
    near_ref, late_table_ref, window, cols, blocks, semaphores,
):
    is_odd, early, first = position()
    window[3:7] = x_ref[...]
    window[0:3] = jnp.where(is_odd, sibling_ref[0:3], next_ref[0:3])
    window[7:10] = jnp.where(is_odd, next_ref[0:3], sibling_ref[0:3])
    zero = jnp.zeros((32, 128), BF16)
    left, right = [], []
    for pair in (3, 4):
        from_sibling, from_next = sibling_ref[pair], next_ref[pair]
        before = jnp.where(is_odd, from_sibling, from_next)
        after = jnp.where(is_odd, from_next, from_sibling)
        left += [before[:, :128], before[:, 128:]]
        right += [after[:, :128], after[:, 128:]]
    rows = []
    for j in range(4):
        row = [left[j - k] if k <= j else zero for k in range(4)]
        row += [right[j + k] if k <= 3 - j else zero for k in range(4)]
        rows.append(jnp.concatenate(row, axis=1))
    matrices = stacked([leaf_ref[k] for k in range(8)], 0)
    coupled = halves(dot(jnp.concatenate(rows, axis=0), matrices))
    field = fourths(own_ref[...])

    def add_far(j, table_ref):
        leaf_part = dot(coupled[32 * j : 32 * j + 32], stacked([basis_ref[j]], 0))
        both = dot(field, table_ref[:, 256 * j : 256 * j + 256])
        return leaf_part + both[:32] + both[32:]

    @pl.when(early)
    def _():
        for j in range(4):
            total = begun_ref[j] + add_far(j, early_table_ref)
            for slot, (leaf, t) in enumerate(MISSING):
                if leaf == j:
                    total += dot_nt(window[t], rest_ref[slot])
            near_ref[j] = total

    @pl.when(jnp.logical_not(early))
    def _():
        copies = load_near(cols_hbm, blocks_hbm, cols, blocks, semaphores)
        expand(transfer_ref, basis_ref, late_table_ref)
        near_all(window, cols, blocks, copies, near_ref, first)
        for j in range(4):
            near_ref[j] += add_far(j, late_table_ref)


def product_kernel(
    near_ref, even_ref, odd_ref, node_ref, early_table_ref, late_table_ref, out_hbm, out, semaphores
):
    _, early, _ = position()
    is_odd = lax.axis_index("leaf") % 2 == 1
    given = even_ref[0].astype(F32) + odd_ref[0].astype(F32)
    row = [jnp.where(is_odd, even_ref[i], odd_ref[i]) for i in (1, 2)]
    row += [jnp.where(is_odd, odd_ref[i], even_ref[i]) for i in (1, 2)]
    beside = dot(jnp.concatenate(row, axis=1), stacked([node_ref[0, k] for k in range(4)], 0))
    field = fourths(given[:, :64] + given[:, 64:] + beside)

    def finish(table_ref):
        copies = []
        for j in range(4):
            both = dot(field, table_ref[:, 256 * j : 256 * j + 256])
            out[j] = near_ref[j] + both[:32] + both[32:]
            copies.append(pltpu.make_async_copy(out.at[j], out_hbm.at[j], semaphores.at[j]))
            copies[-1].start()
        for copy in copies:
            copy.wait()

    @pl.when(early)
    def _():
        finish(early_table_ref)

    @pl.when(jnp.logical_not(early))
    def _():
        finish(late_table_ref)


def call(kernel, out, specs, scratch=(), flops=0, size=0, out_spec=VMEM, aliases=()):
    return pl.pallas_call(
        kernel,
        out_shape=[jax.ShapeDtypeStruct(shape, dtype) for shape, dtype in out],
        in_specs=specs,
        out_specs=out_spec if isinstance(out_spec, list) else [out_spec] * len(out),
        input_output_aliases=dict(aliases),
        scratch_shapes=list(scratch),
        compiler_params=pltpu.CompilerParams(vmem_limit_bytes=16 << 20),
        cost_estimate=pl.CostEstimate(flops=flops, bytes_accessed=size, transcendentals=0),
    )


def in_hbm(*arrays):
    return [pltpu.with_memory_space_constraint(array, pltpu.HBM) for array in arrays]


def permute(value, partner):
    members = lax.axis_size(AXES)
    return lax.ppermute(value, AXES, [(i, partner(i) % members) for i in range(members)])


def local(
    input_point_values,
    leaf_cluster_basis,
    near_blocks,
    near_cols,
    leaf_transfer,
    leaf_coupling,
    node_coupling,
    level_transfer,
    level_coupling,
):
    block = lax.axis_size("near")
    x, basis, transfer, chunk, package, other_package, level, coupling, leaf, node = call(
        moments_kernel,
        [
            ((4, 32, 256), BF16),
            ((4, 64, 256), BF16),
            ((4, 64, 64), BF16),
            ((block, 32, 128), BF16),
            ((5, 32, 256), BF16),
            ((5, 32, 256), BF16),
            ((3, 2, 64, 64), BF16),
            ((3, 4, 64, 64), BF16),
            ((8, 64, 64), BF16),
            ((1, 4, 64, 64), BF16),
        ],
        [HBM] * 7,
        [pltpu.SemaphoreType.DMA((7,))],
    )(
        *in_hbm(
            input_point_values,
            leaf_cluster_basis,
            leaf_transfer,
            level_transfer,
            level_coupling,
            leaf_coupling,
            node_coupling,
        )
    )
    begun, rest, early_table = call(
        early_kernel,
        [((4, 32, 256), F32), ((12, 256, 256), BF16), ((128, 1024), BF16)],
        [VMEM] * 3 + [HBM] * 2,
        [
            pltpu.VMEM((10, 32, 256), BF16),
            pltpu.SMEM((4, 7), jnp.int32),
            pltpu.VMEM((4, 7, 256, 256), BF16),
            pltpu.SemaphoreType.DMA((5,)),
        ],
    )(x, transfer, basis, *in_hbm(near_cols, near_blocks))
    chunk, begun, package, other_package = lax.optimization_barrier(
        (chunk, begun, package, other_package)
    )
    nodes = lax.all_to_all(chunk, "near", 0, 0)
    after = permute(other_package, lambda i: i + 1 if i % 2 else i - 1)
    sibling = permute(package, lambda i: i ^ 1)
    even, odd, own = call(
        levels_kernel,
        [((3, 32, 128), BF16), ((3, 32, 128), BF16), ((32, 64), F32)],
        [VMEM] * 4,
        [
            pltpu.VMEM((8, 32, 128), BF16),
            pltpu.VMEM((4, 32, 128), BF16),
            pltpu.VMEM((2, 32, 128), BF16),
        ],
    )(nodes, level, coupling, node)
    odd = permute(odd, lambda i: i + block if i // block % 2 else i - block)
    even = permute(even, lambda i: i - block if i // block % 2 else i + block)
    near, late_table = call(
        near_kernel,
        [((4, 32, 256), F32), ((128, 1024), BF16)],
        [VMEM] * 10 + [HBM] * 2,
        [
            pltpu.VMEM((10, 32, 256), BF16),
            pltpu.SMEM((4, 7), jnp.int32),
            pltpu.VMEM((4, 7, 256, 256), BF16),
            pltpu.SemaphoreType.DMA((5,)),
        ],
        flops=200_000_000,
        size=4_000_000,
    )(
        x,
        sibling,
        after,
        own,
        leaf,
        transfer,
        basis,
        begun,
        rest,
        early_table,
        *in_hbm(near_cols, near_blocks),
    )
    (out,) = call(
        product_kernel,
        [((4, 32, 256), F32)],
        [VMEM] * 6,
        [pltpu.VMEM((4, 32, 256), F32), pltpu.SemaphoreType.DMA((4,))],
        out_spec=HBM,
    )(near, even, odd, node, early_table, late_table)
    return out


def solution(mesh):
    spread = P(AXES)
    placed = (spread, spread, spread, spread, spread, P(), spread, P(), P())
    return jax.shard_map(
        local, mesh=mesh, in_specs=placed, out_specs=spread, check_vma=False
    )
```

time: 41.4 us -> 36.9 us (0.89)
  starting transfers between devices: 29.6 us -> 23.6 us
  waiting for transfers between devices: 1.79 us -> 3.79 us
  Pallas kernels: 9.55 us -> 9.12 us
    ppermute x4, starting transfers between devices: 23.9 us -> 15.3 us  [permute(): lax.ppermute(value, AXES, [(i, partner(i) % members) for i in range(membe...]
    all_to_all x1, waiting for transfers between devices: 0.01 us -> 3.58 us  [local(): nodes = lax.all_to_all(chunk, 'near', 0, 0)]
    all_to_all x1, starting transfers between devices: 5.72 us -> 8.25 us  [local(): nodes = lax.all_to_all(chunk, 'near', 0, 0)]
    ppermute x4, waiting for transfers between devices: 1.79 us -> 0.21 us  [permute(): lax.ppermute(value, AXES, [(i, partner(i) % members) for i in range(membe...]
    pallas_call x5 -> x4, Pallas kernels: 8.13 us -> 6.99 us  [the longest x1 3.66 us: local(): call(early_kernel, [((4, 32, 256), F32), ((12, 256, 256), BF16), ((128, 1...]
    pallas_call x1, Pallas kernels: 1.42 us -> 2.13 us  [local(): call(moments_kernel, [((4, 32, 256), BF16), ((4, 64, 256), BF16), ((4, 64...]
  transfers between devices with their start and end apart: 5 -> 5, of which waited for: 1 -> 2; matrix products, arithmetic and copies ran while one was open for 0% -> 0% of each run, Pallas kernels for 15% -> 6%
where the time goes in v3:
time: 36.9 us; the launch traced here: 36.6 us
  starting transfers between devices  23.6 us (64%)
  Pallas kernels  9.12 us (25%)
  waiting for transfers between devices  3.79 us (10%)
    ppermute x4, starting transfers between devices, permute(): lax.ppermute(value, AXES, [(i, partner(i) % members) for i in range(membe...  15.3 us
    all_to_all x1, starting transfers between devices, local(): nodes = lax.all_to_all(chunk, 'near', 0, 0)  8.25 us
    pallas_call x1, Pallas kernels, local(): call(early_kernel, [((4, 32, 256), F32), ((12, 256, 256), BF16), ((128, 1...  3.66 us
    all_to_all x1, waiting for transfers between devices, local(): nodes = lax.all_to_all(chunk, 'near', 0, 0)  3.58 us
    pallas_call x1, Pallas kernels, local(): call(moments_kernel, [((4, 32, 256), BF16), ((4, 64, 256), BF16), ((4, 64...  2.13 us
    pallas_call x1, Pallas kernels, local(): call(levels_kernel, [((3, 32, 128), BF16), ((3, 32, 128), BF16), ((32, 64...  1.28 us
    pallas_call x1, Pallas kernels, local(): call(product_kernel, [((4, 32, 256), F32)], [VMEM] * 6, [pltpu.VMEM((4, 3...  1.04 us
    pallas_call x1, Pallas kernels, local(): call(near_kernel, [((4, 32, 256), F32), ((128, 1024), BF16)], [VMEM] * 10...  1.01 us
  transfers between devices with their start and end apart: 5, of which 2 were waited for; matrix products, arithmetic and copies ran while one was open for 0% of the time, Pallas kernels for 6%

profile of v3, /device:TPU:1, one launch (start us, length us, event | category | flops | bytes accessed | tf_op | source)
XLA Modules:
  0.0 36.6 jit_solution(2865699351367650749)
XLA Ops:
  0.0 2.1 %shard_map.91 = (bf16[4,32,256]{2,1,0:T(8,128)(2,1)S(1)}, bf16[4,64,256]{2,1,0:T(8,128)(2,1)S(1)}, bf16[4,64,64]{2,1,0:T(8,128)(2,1)S(1)}, bf16[16,32,128]{2,1,0...) custom-call(bf16[4,32,256]{2,1,0:T(8,128)(2,1)} %x_hbm.1, ...), custom_call_target="tpu_custom_call" | custom-call | tf_op jit(solution)/shard_map/pallas_call | solution.py:323
  2.1 3.7 %shard_map.92 = (f32[4,32,256]{2,1,0:T(8,128)S(1)}, bf16[12,256,256]{2,1,0:T(8,128)(2,1)S(1)}, bf16[128,1024]{1,0:T(8,128)(2,1)S(1)}) custom-call(bf16[4,32,256]{2,1,0:T(8,128)(2,1)S(1)} %get-tuple-element.27.x_ref, bf16[4,64,64]{2,1,0:T(8,128)(2,1)S(1)} %get-tuple-element.29.transfer_ref, bf16[4,64,256]{2,1,0:T(8,128)(2,1)S(1)} %get-tuple-element.30.basis_ref, ...), custom_call_target="tpu_custom_call" | custom-call | tf_op jit(solution)/shard_map/pallas_call | solution.py:350
  5.8 8.2 %all-to-all-start = ((bf16[16,32,128]{2,1,0:T(8,128)(2,1)}), bf16[16,32,128]{2,1,0:T(8,128)(2,1)S(1)}, u32[]{:S(2)}, u32[]{:S(2)}) async-start(bf16[16,32,128]{2,1,0:T(8,128)(2,1)} %get-tuple-element.36), calls=%async_computation | async-start | bytes 262144 | tf_op jit(solution)/shard_map/all_to_all | solution.py:364
  14.1 2.0 %collective-permute-start = (bf16[5,32,256]{2,1,0:T(8,128)(2,1)S(1)}, bf16[5,32,256]{2,1,0:T(8,128)(2,1)S(1)}, u32[]{:S(2)}, u32[]{:S(2)}) collective-permute-start(bf16[5,32,256]{2,1,0:T(8,128)(2,1)S(1)} %get-tuple-element.34), channel_id=1, source_target_pairs={{0,1},{1,0},{2,3},{3,2},{4,5},{5,4},{6,7},{7,6},{8,9},{9,8},{10,11... | collective-permute-start | bytes 245768 | tf_op jit(solution)/shard_map/ppermute | solution.py:308
  16.1 3.6 %collective-permute-start.1 = (bf16[5,32,256]{2,1,0:T(8,128)(2,1)S(1)}, bf16[5,32,256]{2,1,0:T(8,128)(2,1)S(1)}, u32[]{:S(2)}, u32[]{:S(2)}) collective-permute-start(bf16[5,32,256]{2,1,0:T(8,128)(2,1)S(1)} %get-tuple-element.35), channel_id=1, source_target_pairs={{0,511},{1,2},{2,1},{3,4},{4,3},{5,6},{6,5},{7,8},{8,7},{9,10},{10... | collective-permute-start | bytes 245768 | tf_op jit(solution)/shard_map/ppermute | solution.py:308
  19.7 3.6 %all-to-all-done.nodes_ref = bf16[16,32,128]{2,1,0:T(8,128)(2,1)S(1)} async-done(((bf16[16,32,128]{2,1,0:T(8,128)(2,1)}), bf16[16,32,128]{2,1,0:T(8,128)(2,1)S(1)}, u32[]{:S(2)}, u32[]{:S(2)}) %all-to-all-start) | async-done | bytes 131104 | tf_op jit(solution)/shard_map/all_to_all | solution.py:364
  23.2 1.3 %shard_map.93 = (bf16[3,32,128]{2,1,0:T(8,128)(2,1)S(1)}, bf16[3,32,128]{2,1,0:T(8,128)(2,1)S(1)}, f32[32,64]{1,0:T(8,128)S(1)}) custom-call(bf16[16,32,128]{2,1,0:T(8,128)(2,1)S(1)} %all-to-all-done.nodes_ref, bf16[3,2,64,64]{3,2,1,0:T(8,128)(2,1)S(1)} %get-tuple-element.37.level_ref, bf16[3,4,64,64]{3,2,1,0:T(8,128)(2,1)S(1)} %get-tuple-element.38.coupling_ref, ...), custom_call_target="tpu_custom_call" | custom-call | tf_op jit(solution)/shard_map/pallas_call | solution.py:367
  24.5 3.1 %collective-permute-start.2 = (bf16[3,32,128]{2,1,0:T(8,128)(2,1)S(1)}, bf16[3,32,128]{2,1,0:T(8,128)(2,1)S(1)}, u32[]{:S(2)}, u32[]{:S(2)}) collective-permute-start(bf16[3,32,128]{2,1,0:T(8,128)(2,1)S(1)} %get-tuple-element.46), channel_id=1, source_target_pairs={{0,16},{1,17},{2,18},{3,19},{4,20},{5,21},{6,22},{7,23},{8,24},{9,... | collective-permute-start | bytes 73736 | tf_op jit(solution)/shard_map/ppermute | solution.py:308
  27.6 6.6 %collective-permute-start.3 = (bf16[3,32,128]{2,1,0:T(8,128)(2,1)S(1)}, bf16[3,32,128]{2,1,0:T(8,128)(2,1)S(1)}, u32[]{:S(2)}, u32[]{:S(2)}) collective-permute-start(bf16[3,32,128]{2,1,0:T(8,128)(2,1)S(1)} %get-tuple-element.47), channel_id=1, source_target_pairs={{0,496},{1,497},{2,498},{3,499},{4,500},{5,501},{6,502},{7,503},{8... | collective-permute-start | bytes 73736 | tf_op jit(solution)/shard_map/ppermute | solution.py:308
  34.3 0.0 collective-permute-done.sibling_ref
  34.3 0.0 collective-permute-done.1.next_ref
  34.3 1.0 %shard_map.94 = (f32[4,32,256]{2,1,0:T(8,128)S(1)}, bf16[128,1024]{1,0:T(8,128)(2,1)S(1)}) custom-call(bf16[4,32,256]{2,1,0:T(8,128)(2,1)S(1)} %get-tuple-element.27.x_ref, bf16[5,32,256]{2,1,0:T(8,128)(2,1)S(1)} %collective-permute-done.sibling_ref, bf16[5,32,256]{2,1,0:T(8,128)(2,1)S(1)} %collective-permute-done.1.next_ref, ...), custom_call_target="tpu_custom_call" | custom-call | flops 200000000 | bytes 4000000 | tf_op jit(solution)/shard_map/pallas_call | solution.py:379
  35.3 0.0 collective-permute-done.2.even_ref
  35.3 0.2 collective-permute-done.3.odd_ref
  35.5 1.0 %shard_map.95 = f32[4,32,256]{2,1,0:T(8,128)} custom-call(f32[4,32,256]{2,1,0:T(8,128)S(1)} %get-tuple-element.45.near_ref, bf16[3,32,128]{2,1,0:T(8,128)(2,1)S(1)} %collective-permute-done.2.even_ref, bf16[3,32,128]{2,1,0:T(8,128)(2,1)S(1)} %collective-permute-done.3.odd_ref, bf16[1,4,64,64]{3,2,1,0:T(8,128)(2,1)S(1)} %get-tuple-element.39.node_ref, ...), custom_call_target="tpu_custom_call" | custom-call | tf_op jit(solution)/shard_map/pallas_call | solution.py:404
Async XLA Ops:
  5.8 17.4 %all-to-all-start = ((bf16[16,32,128]{2,1,0:T(8,128)(2,1)}), bf16[16,32,128]{2,1,0:T(8,128)(2,1)S(1)}, u32[]{:S(2)}, u32[]{:S(2)}) async-start(bf16[16,32,128]{2,1,0:T(8,128)(2,1)} %get-tuple-element.36), calls=%async_computation | async-start | bytes 262144 | tf_op jit(solution)/shard_map/all_to_all | solution.py:364
  14.1 20.2 %collective-permute-start = (bf16[5,32,256]{2,1,0:T(8,128)(2,1)S(1)}, bf16[5,32,256]{2,1,0:T(8,128)(2,1)S(1)}, u32[]{:S(2)}, u32[]{:S(2)}) collective-permute-start(bf16[5,32,256]{2,1,0:T(8,128)(2,1)S(1)} %get-tuple-element.34), channel_id=1, source_target_pairs={{0,1},{1,0},{2,3},{3,2},{4,5},{5,4},{6,7},{7,6},{8,9},{9,8},{10,11... | collective-permute-start | bytes 245768 | tf_op jit(solution)/shard_map/ppermute | solution.py:308
  16.1 18.2 %collective-permute-start.1 = (bf16[5,32,256]{2,1,0:T(8,128)(2,1)S(1)}, bf16[5,32,256]{2,1,0:T(8,128)(2,1)S(1)}, u32[]{:S(2)}, u32[]{:S(2)}) collective-permute-start(bf16[5,32,256]{2,1,0:T(8,128)(2,1)S(1)} %get-tuple-element.35), channel_id=1, source_target_pairs={{0,511},{1,2},{2,1},{3,4},{4,3},{5,6},{6,5},{7,8},{8,7},{9,10},{10... | collective-permute-start | bytes 245768 | tf_op jit(solution)/shard_map/ppermute | solution.py:308
  24.5 10.8 %collective-permute-start.2 = (bf16[3,32,128]{2,1,0:T(8,128)(2,1)S(1)}, bf16[3,32,128]{2,1,0:T(8,128)(2,1)S(1)}, u32[]{:S(2)}, u32[]{:S(2)}) collective-permute-start(bf16[3,32,128]{2,1,0:T(8,128)(2,1)S(1)} %get-tuple-element.46), channel_id=1, source_target_pairs={{0,16},{1,17},{2,18},{3,19},{4,20},{5,21},{6,22},{7,23},{8,24},{9,... | collective-permute-start | bytes 73736 | tf_op jit(solution)/shard_map/ppermute | solution.py:308
  27.6 7.9 %collective-permute-start.3 = (bf16[3,32,128]{2,1,0:T(8,128)(2,1)S(1)}, bf16[3,32,128]{2,1,0:T(8,128)(2,1)S(1)}, u32[]{:S(2)}, u32[]{:S(2)}) collective-permute-start(bf16[3,32,128]{2,1,0:T(8,128)(2,1)S(1)} %get-tuple-element.47), channel_id=1, source_target_pairs={{0,496},{1,497},{2,498},{3,499},{4,500},{5,501},{6,502},{7,503},{8... | collective-permute-start | bytes 73736 | tf_op jit(solution)/shard_map/ppermute | solution.py:308

commit v4 on v3

--- a/solution.py
+++ b/solution.py
@@ -45,13 +45,14 @@
 
 def moments_kernel(
     x_hbm, basis_hbm, transfer_hbm, level_hbm, coupling_hbm, leaf_hbm, node_hbm,
-    x_ref, basis_ref, transfer_ref, chunk_ref, sibling_ref, next_ref, level_ref, coupling_ref,
-    leaf_ref, node_ref, semaphores,
-):
-    odd = lax.axis_index("near") % 2
+    x_ref, basis_ref, transfer_ref, chunk_hbm, sibling_ref, next_ref, level_ref, table_ref,
+    leaf_ref, node_ref, coupling, chunk, semaphores,
+):
+    near = lax.axis_index("near")
+    odd = near % 2
     copies = load(
         (x_hbm, basis_hbm, transfer_hbm, level_hbm, coupling_hbm, node_hbm, leaf_hbm),
-        (x_ref, basis_ref, transfer_ref, level_ref, coupling_ref, node_ref, leaf_ref),
+        (x_ref, basis_ref, transfer_ref, level_ref, coupling, node_ref, leaf_ref),
         semaphores,
     )
     copies[0].wait()
@@ -60,18 +61,31 @@
     copies[2].wait()
     weights = stacked([transfer_ref[j] for j in range(4)], 0)
     moments = halves(dot(jnp.concatenate(parts, axis=1), weights))
-    for j in range(chunk_ref.shape[0]):
-        chunk_ref[j] = moments
+    for j in range(chunk.shape[0]):
+        chunk[j] = moments
+    send = pltpu.make_async_copy(chunk, chunk_hbm, semaphores.at[7])
+    send.start()
+    for copy in copies[3:]:
+        copy.wait()
+    down = None
+    for c in range(3):
+        chosen = level_ref[c, (near >> c) % 2]
+        matrices = jnp.concatenate([coupling[c, k] for k in range(4)], axis=0)
+        if c == 0:
+            down = chosen
+        else:
+            down = halves(dot(down, chosen if c == 1 else stacked([chosen], 0)))
+            matrices = jnp.concatenate([matrices, matrices], axis=1)
+        table_ref[256 * c : 256 * c + 256] = halves(dot_nt(matrices, down))
     for ref, first in ((sibling_ref, 1 - odd), (next_ref, odd)):
         ref[0:3] = x_ref[pl.ds(first, 3)]
         ref[3] = jnp.concatenate(parts[:2], axis=1)
         ref[4] = jnp.concatenate(parts[2:], axis=1)
-    for copy in copies[3:]:
-        copy.wait()
+    send.wait()
 
 
 def levels_kernel(
-    nodes_ref, level_ref, coupling_ref, node_ref, even_ref, odd_ref, own_ref,
+    nodes_ref, level_ref, table_ref, node_ref, first_ref, odd_ref, even_ref, own_ref,
     chips, quads, octets,
 ):
     near = lax.axis_index("near")
@@ -113,20 +127,7 @@
         )
         for target in targets
     ]
-    down, tables = None, []
-    for c in range(3):
-        chosen = level_ref[c, (near >> c) % 2]
-        if c == 0:
-            down = chosen
-        else:
-            down = halves(dot(down, chosen if c == 1 else stacked([chosen], 0)))
-        matrices = jnp.concatenate([coupling_ref[c, k] for k in range(4)], axis=0)
-        if c == 0:
-            tables.append(dot_nt(matrices, down))
-        else:
-            tables.append(dot_nt(jnp.concatenate([matrices, matrices], axis=1), down))
-    table = halves(jnp.concatenate(tables, axis=0))
-    table = stacked([table[64 * i : 64 * i + 64] for i in range(12)], 0)
+    table = stacked([table_ref[64 * i : 64 * i + 64] for i in range(12)], 0)
     both = dot(jnp.concatenate(rows, axis=0), table)
     field = both[:, :64] + both[:, 64:]
     beside = jnp.concatenate(partners(nodes_ref, near, 0), axis=1)
@@ -136,6 +137,11 @@
     for i in range(3):
         even_ref[i] = jnp.where(is_odd, before[i], after[i])
         odd_ref[i] = jnp.where(is_odd, after[i], before[i])
+        first_ref[i] = before[i]
+    zero = jnp.zeros((32, 128), BF16)
+    odd_ref[3] = zero
+    first_ref[3] = zero
+    first_ref[4] = zero
 
 
 def near_all(window, cols, blocks, copies, near_ref, first):
@@ -257,13 +263,15 @@
 
 
 def product_kernel(
-    near_ref, even_ref, odd_ref, node_ref, early_table_ref, late_table_ref, out_hbm, out, semaphores
+    near_ref, first_ref, odd_ref, even_ref, node_ref, early_table_ref, late_table_ref, out_hbm,
+    out, semaphores,
 ):
     _, early, _ = position()
     is_odd = lax.axis_index("leaf") % 2 == 1
-    given = even_ref[0].astype(F32) + odd_ref[0].astype(F32)
-    row = [jnp.where(is_odd, even_ref[i], odd_ref[i]) for i in (1, 2)]
-    row += [jnp.where(is_odd, odd_ref[i], even_ref[i]) for i in (1, 2)]
+    even = [first_ref[i] + even_ref[i] for i in range(3)]
+    given = even[0].astype(F32) + odd_ref[0].astype(F32)
+    row = [jnp.where(is_odd, even[i], odd_ref[i]) for i in (1, 2)]
+    row += [jnp.where(is_odd, odd_ref[i], even[i]) for i in (1, 2)]
     beside = dot(jnp.concatenate(row, axis=1), stacked([node_ref[0, k] for k in range(4)], 0))
     field = fourths(given[:, :64] + given[:, 64:] + beside)
 
@@ -303,9 +311,10 @@
     return [pltpu.with_memory_space_constraint(array, pltpu.HBM) for array in arrays]
 
 
-def permute(value, partner):
+def permute(value, partner, taking=lambda i: True):
     members = lax.axis_size(AXES)
-    return lax.ppermute(value, AXES, [(i, partner(i) % members) for i in range(members)])
+    pairs = [(i, partner(i) % members) for i in range(members) if taking(i)]
+    return lax.ppermute(value, AXES, pairs)
 
 
 def local(
@@ -330,12 +339,17 @@
             ((5, 32, 256), BF16),
             ((5, 32, 256), BF16),
             ((3, 2, 64, 64), BF16),
-            ((3, 4, 64, 64), BF16),
+            ((768, 128), BF16),
             ((8, 64, 64), BF16),
             ((1, 4, 64, 64), BF16),
         ],
         [HBM] * 7,
-        [pltpu.SemaphoreType.DMA((7,))],
+        [
+            pltpu.VMEM((3, 4, 64, 64), BF16),
+            pltpu.VMEM((block, 32, 128), BF16),
+            pltpu.SemaphoreType.DMA((8,)),
+        ],
+        out_spec=[VMEM] * 3 + [HBM] + [VMEM] * 6,
     )(
         *in_hbm(
             input_point_values,
@@ -364,9 +378,9 @@
     nodes = lax.all_to_all(chunk, "near", 0, 0)
     after = permute(other_package, lambda i: i + 1 if i % 2 else i - 1)
     sibling = permute(package, lambda i: i ^ 1)
-    even, odd, own = call(
+    first, odd, even, own = call(
         levels_kernel,
-        [((3, 32, 128), BF16), ((3, 32, 128), BF16), ((32, 64), F32)],
+        [((5, 32, 128), BF16), ((4, 32, 128), BF16), ((3, 32, 128), BF16), ((32, 64), F32)],
         [VMEM] * 4,
         [
             pltpu.VMEM((8, 32, 128), BF16),
@@ -374,8 +388,15 @@
             pltpu.VMEM((2, 32, 128), BF16),
         ],
     )(nodes, level, coupling, node)
+
+    def to_first(i):
+        return i // block == 1 and i % block > 0
+
+    first = permute(first, lambda i: i - block, to_first)
     odd = permute(odd, lambda i: i + block if i // block % 2 else i - block)
-    even = permute(even, lambda i: i - block if i // block % 2 else i + block)
+    even = permute(
+        even, lambda i: i - block if i // block % 2 else i + block, lambda i: not to_first(i)
+    )
     near, late_table = call(
         near_kernel,
         [((4, 32, 256), F32), ((128, 1024), BF16)],
@@ -404,10 +425,10 @@
     (out,) = call(
         product_kernel,
         [((4, 32, 256), F32)],
-        [VMEM] * 6,
+        [VMEM] * 7,
         [pltpu.VMEM((4, 32, 256), F32), pltpu.SemaphoreType.DMA((4,))],
         out_spec=HBM,
-    )(near, even, odd, node, early_table, late_table)
+    )(near, first, odd, even, node, early_table, late_table)
     return out
 
 

time: 36.9 us -> 36.3 us (0.984)
  starting transfers between devices: 23.6 us -> 23.2 us
    ppermute x4 -> x5, starting transfers between devices: 15.3 us -> 14.9 us  [permute(): return lax.ppermute(value, AXES, pairs)]
  transfers between devices with their start and end apart: 5 -> 6, of which waited for: 2 -> 1; matrix products, arithmetic and copies ran while one was open for 0% -> 0% of each run, Pallas kernels for 6% -> 6%
where the time goes in v4:
time: 36.3 us; the launch traced here: 35.7 us
  starting transfers between devices  23.2 us (64%)
  Pallas kernels  8.83 us (24%)
  waiting for transfers between devices  3.59 us (10%)
    ppermute x5, starting transfers between devices, permute(): return lax.ppermute(value, AXES, pairs)  14.9 us
    all_to_all x1, starting transfers between devices, local(): nodes = lax.all_to_all(chunk, 'near', 0, 0)  8.25 us
    pallas_call x1, Pallas kernels, local(): call(early_kernel, [((4, 32, 256), F32), ((12, 256, 256), BF16), ((128, 1...  3.66 us
    all_to_all x1, waiting for transfers between devices, local(): nodes = lax.all_to_all(chunk, 'near', 0, 0)  3.58 us
    pallas_call x1, Pallas kernels, local(): call(moments_kernel, [((4, 32, 256), BF16), ((4, 64, 256), BF16), ((4, 64...  2.14 us
    pallas_call x1, Pallas kernels, local(): call(product_kernel, [((4, 32, 256), F32)], [VMEM] * 7, [pltpu.VMEM((4, 3...  1.04 us
    pallas_call x1, Pallas kernels, local(): call(near_kernel, [((4, 32, 256), F32), ((128, 1024), BF16)], [VMEM] * 10...  1.01 us
    pallas_call x1, Pallas kernels, local(): call(levels_kernel, [((5, 32, 128), BF16), ((4, 32, 128), BF16), ((3, 32,...  0.98 us
  transfers between devices with their start and end apart: 6, of which 1 were waited for; matrix products, arithmetic and copies ran while one was open for 0% of the time, Pallas kernels for 6%

profile of v4, /device:TPU:1, one launch (start us, length us, event | category | flops | bytes accessed | tf_op | source)
XLA Modules:
  0.0 35.7 jit_solution(14821983385459790075)
XLA Ops:
  0.0 2.1 %shard_map.91 = (bf16[4,32,256]{2,1,0:T(8,128)(2,1)S(1)}, bf16[4,64,256]{2,1,0:T(8,128)(2,1)S(1)}, bf16[4,64,64]{2,1,0:T(8,128)(2,1)S(1)}, bf16[16,32,128]{2,1,0...) custom-call(bf16[4,32,256]{2,1,0:T(8,128)(2,1)} %x_hbm.1, ...), custom_call_target="tpu_custom_call" | custom-call | tf_op jit(solution)/shard_map/pallas_call | solution.py:332
  2.2 3.7 %shard_map.92 = (f32[4,32,256]{2,1,0:T(8,128)S(1)}, bf16[12,256,256]{2,1,0:T(8,128)(2,1)S(1)}, bf16[128,1024]{1,0:T(8,128)(2,1)S(1)}) custom-call(bf16[4,32,256]{2,1,0:T(8,128)(2,1)S(1)} %get-tuple-element.28.x_ref, bf16[4,64,64]{2,1,0:T(8,128)(2,1)S(1)} %get-tuple-element.30.transfer_ref, bf16[4,64,256]{2,1,0:T(8,128)(2,1)S(1)} %get-tuple-element.31.basis_ref, ...), custom_call_target="tpu_custom_call" | custom-call | tf_op jit(solution)/shard_map/pallas_call | solution.py:364
  5.8 8.2 %all-to-all-start = ((bf16[16,32,128]{2,1,0:T(8,128)(2,1)}), bf16[16,32,128]{2,1,0:T(8,128)(2,1)S(1)}, u32[]{:S(2)}, u32[]{:S(2)}) async-start(bf16[16,32,128]{2,1,0:T(8,128)(2,1)} %get-tuple-element.37), calls=%async_computation | async-start | bytes 262144 | tf_op jit(solution)/shard_map/all_to_all | solution.py:378
  14.1 2.0 %collective-permute-start = (bf16[5,32,256]{2,1,0:T(8,128)(2,1)S(1)}, bf16[5,32,256]{2,1,0:T(8,128)(2,1)S(1)}, u32[]{:S(2)}, u32[]{:S(2)}) collective-permute-start(bf16[5,32,256]{2,1,0:T(8,128)(2,1)S(1)} %get-tuple-element.35), channel_id=1, source_target_pairs={{0,1},{1,0},{2,3},{3,2},{4,5},{5,4},{6,7},{7,6},{8,9},{9,8},{10,11... | collective-permute-start | bytes 245768 | tf_op jit(solution)/shard_map/ppermute | solution.py:317
  16.1 3.6 %collective-permute-start.1 = (bf16[5,32,256]{2,1,0:T(8,128)(2,1)S(1)}, bf16[5,32,256]{2,1,0:T(8,128)(2,1)S(1)}, u32[]{:S(2)}, u32[]{:S(2)}) collective-permute-start(bf16[5,32,256]{2,1,0:T(8,128)(2,1)S(1)} %get-tuple-element.36), channel_id=1, source_target_pairs={{0,511},{1,2},{2,1},{3,4},{4,3},{5,6},{6,5},{7,8},{8,7},{9,10},{10... | collective-permute-start | bytes 245768 | tf_op jit(solution)/shard_map/ppermute | solution.py:317
  19.7 3.6 %all-to-all-done.nodes_ref = bf16[16,32,128]{2,1,0:T(8,128)(2,1)S(1)} async-done(((bf16[16,32,128]{2,1,0:T(8,128)(2,1)}), bf16[16,32,128]{2,1,0:T(8,128)(2,1)S(1)}, u32[]{:S(2)}, u32[]{:S(2)}) %all-to-all-start) | async-done | bytes 131104 | tf_op jit(solution)/shard_map/all_to_all | solution.py:378
  23.2 1.0 %shard_map.93 = (bf16[5,32,128]{2,1,0:T(8,128)(2,1)S(1)}, bf16[4,32,128]{2,1,0:T(8,128)(2,1)S(1)}, bf16[3,32,128]{2,1,0:T(8,128)(2,1)S(1)}, f32[32,64]{1,0:T(8,128)S(1)}) custom-call(bf16[16,32,128]{2,1,0:T(8,128)(2,1)S(1)} %all-to-all-done.nodes_ref, bf16[3,2,64,64]{3,2,1,0:T(8,128)(2,1)S(1)} %get-tuple-element.38.level_ref, ...), custom_call_target="tpu_custom_call" | custom-call | tf_op jit(solution)/shard_map/pallas_call | solution.py:381
  24.2 1.3 %collective-permute-start.2 = (bf16[5,32,128]{2,1,0:T(8,128)(2,1)S(1)}, bf16[5,32,128]{2,1,0:T(8,128)(2,1)S(1)}, u32[]{:S(2)}, u32[]{:S(2)}) collective-permute-start(bf16[5,32,128]{2,1,0:T(8,128)(2,1)S(1)} %get-tuple-element.47), channel_id=1, source_target_pairs={{17,1},{18,2},{19,3},{20,4},{21,5},{22,6},{23,7},{24,8},{25,9},{26... | collective-permute-start | bytes 122888 | tf_op jit(solution)/shard_map/ppermute | solution.py:317
  25.5 6.7 %collective-permute-start.3 = (bf16[4,32,128]{2,1,0:T(8,128)(2,1)S(1)}, bf16[4,32,128]{2,1,0:T(8,128)(2,1)S(1)}, u32[]{:S(2)}, u32[]{:S(2)}) collective-permute-start(bf16[4,32,128]{2,1,0:T(8,128)(2,1)S(1)} %get-tuple-element.48), channel_id=1, source_target_pairs={{0,496},{1,497},{2,498},{3,499},{4,500},{5,501},{6,502},{7,503},{8... | collective-permute-start | bytes 98312 | tf_op jit(solution)/shard_map/ppermute | solution.py:317
  32.3 1.3 %collective-permute-start.4 = (bf16[3,32,128]{2,1,0:T(8,128)(2,1)S(1)}, bf16[3,32,128]{2,1,0:T(8,128)(2,1)S(1)}, u32[]{:S(2)}, u32[]{:S(2)}) collective-permute-start(bf16[3,32,128]{2,1,0:T(8,128)(2,1)S(1)} %get-tuple-element.49), channel_id=1, source_target_pairs={{0,16},{1,17},{2,18},{3,19},{4,20},{5,21},{6,22},{7,23},{8,24},{9,... | collective-permute-start | bytes 73736 | tf_op jit(solution)/shard_map/ppermute | solution.py:317
  33.6 0.0 collective-permute-done.sibling_ref
  33.6 0.0 collective-permute-done.1.next_ref
  33.6 1.0 %shard_map.94 = (f32[4,32,256]{2,1,0:T(8,128)S(1)}, bf16[128,1024]{1,0:T(8,128)(2,1)S(1)}) custom-call(bf16[4,32,256]{2,1,0:T(8,128)(2,1)S(1)} %get-tuple-element.28.x_ref, bf16[5,32,256]{2,1,0:T(8,128)(2,1)S(1)} %collective-permute-done.sibling_ref, bf16[5,32,256]{2,1,0:T(8,128)(2,1)S(1)} %collective-permute-done.1.next_ref, ...), custom_call_target="tpu_custom_call" | custom-call | flops 200000000 | bytes 4000000 | tf_op jit(solution)/shard_map/pallas_call | solution.py:400
  34.6 0.0 collective-permute-done.4.even_ref
  34.6 0.0 collective-permute-done.3.odd_ref
  34.6 0.0 collective-permute-done.2.first_ref
  34.6 1.0 %shard_map.95 = f32[4,32,256]{2,1,0:T(8,128)} custom-call(f32[4,32,256]{2,1,0:T(8,128)S(1)} %get-tuple-element.46.near_ref, bf16[5,32,128]{2,1,0:T(8,128)(2,1)S(1)} %collective-permute-done.2.first_ref, bf16[4,32,128]{2,1,0:T(8,128)(2,1)S(1)} %collective-permute-done.3.odd_ref, bf16[3,32,128]{2,1,0:T(8,128)(2,1)S(1)} %collective-permute-done.4.even_ref, ...), custom_call_target="tpu_custom_call" | custom-call | tf_op jit(solution)/shard_map/pallas_call | solution.py:425
Async XLA Ops:
  5.8 17.4 %all-to-all-start = ((bf16[16,32,128]{2,1,0:T(8,128)(2,1)}), bf16[16,32,128]{2,1,0:T(8,128)(2,1)S(1)}, u32[]{:S(2)}, u32[]{:S(2)}) async-start(bf16[16,32,128]{2,1,0:T(8,128)(2,1)} %get-tuple-element.37), calls=%async_computation | async-start | bytes 262144 | tf_op jit(solution)/shard_map/all_to_all | solution.py:378
  14.1 19.5 %collective-permute-start = (bf16[5,32,256]{2,1,0:T(8,128)(2,1)S(1)}, bf16[5,32,256]{2,1,0:T(8,128)(2,1)S(1)}, u32[]{:S(2)}, u32[]{:S(2)}) collective-permute-start(bf16[5,32,256]{2,1,0:T(8,128)(2,1)S(1)} %get-tuple-element.35), channel_id=1, source_target_pairs={{0,1},{1,0},{2,3},{3,2},{4,5},{5,4},{6,7},{7,6},{8,9},{9,8},{10,11... | collective-permute-start | bytes 245768 | tf_op jit(solution)/shard_map/ppermute | solution.py:317
  16.1 17.5 %collective-permute-start.1 = (bf16[5,32,256]{2,1,0:T(8,128)(2,1)S(1)}, bf16[5,32,256]{2,1,0:T(8,128)(2,1)S(1)}, u32[]{:S(2)}, u32[]{:S(2)}) collective-permute-start(bf16[5,32,256]{2,1,0:T(8,128)(2,1)S(1)} %get-tuple-element.36), channel_id=1, source_target_pairs={{0,511},{1,2},{2,1},{3,4},{4,3},{5,6},{6,5},{7,8},{8,7},{9,10},{10... | collective-permute-start | bytes 245768 | tf_op jit(solution)/shard_map/ppermute | solution.py:317
  24.2 10.4 %collective-permute-start.2 = (bf16[5,32,128]{2,1,0:T(8,128)(2,1)S(1)}, bf16[5,32,128]{2,1,0:T(8,128)(2,1)S(1)}, u32[]{:S(2)}, u32[]{:S(2)}) collective-permute-start(bf16[5,32,128]{2,1,0:T(8,128)(2,1)S(1)} %get-tuple-element.47), channel_id=1, source_target_pairs={{17,1},{18,2},{19,3},{20,4},{21,5},{22,6},{23,7},{24,8},{25,9},{26... | collective-permute-start | bytes 122888 | tf_op jit(solution)/shard_map/ppermute | solution.py:317
  25.5 9.1 %collective-permute-start.3 = (bf16[4,32,128]{2,1,0:T(8,128)(2,1)S(1)}, bf16[4,32,128]{2,1,0:T(8,128)(2,1)S(1)}, u32[]{:S(2)}, u32[]{:S(2)}) collective-permute-start(bf16[4,32,128]{2,1,0:T(8,128)(2,1)S(1)} %get-tuple-element.48), channel_id=1, source_target_pairs={{0,496},{1,497},{2,498},{3,499},{4,500},{5,501},{6,502},{7,503},{8... | collective-permute-start | bytes 98312 | tf_op jit(solution)/shard_map/ppermute | solution.py:317
  32.3 2.3 %collective-permute-start.4 = (bf16[3,32,128]{2,1,0:T(8,128)(2,1)S(1)}, bf16[3,32,128]{2,1,0:T(8,128)(2,1)S(1)}, u32[]{:S(2)}, u32[]{:S(2)}) collective-permute-start(bf16[3,32,128]{2,1,0:T(8,128)(2,1)S(1)} %get-tuple-element.49), channel_id=1, source_target_pairs={{0,16},{1,17},{2,18},{3,19},{4,20},{5,21},{6,22},{7,23},{8,24},{9,... | collective-permute-start | bytes 73736 | tf_op jit(solution)/shard_map/ppermute | solution.py:317

commit v5 on v4

--- a/solution.py
+++ b/solution.py
@@ -137,11 +137,7 @@
     for i in range(3):
         even_ref[i] = jnp.where(is_odd, before[i], after[i])
         odd_ref[i] = jnp.where(is_odd, after[i], before[i])
-        first_ref[i] = before[i]
-    zero = jnp.zeros((32, 128), BF16)
-    odd_ref[3] = zero
-    first_ref[3] = zero
-    first_ref[4] = zero
+        first_ref[i] = jnp.where(is_odd, before[i], after[i])
 
 
 def near_all(window, cols, blocks, copies, near_ref, first):
@@ -380,7 +376,7 @@
     sibling = permute(package, lambda i: i ^ 1)
     first, odd, even, own = call(
         levels_kernel,
-        [((5, 32, 128), BF16), ((4, 32, 128), BF16), ((3, 32, 128), BF16), ((32, 64), F32)],
+        [((3, 32, 128), BF16), ((3, 32, 128), BF16), ((3, 32, 128), BF16), ((32, 64), F32)],
         [VMEM] * 4,
         [
             pltpu.VMEM((8, 32, 128), BF16),
@@ -390,9 +386,9 @@
     )(nodes, level, coupling, node)
 
     def to_first(i):
-        return i // block == 1 and i % block > 0
-
-    first = permute(first, lambda i: i - block, to_first)
+        return i // block == 1 and i % block > 0 or i == 0
+
+    first = permute(first, lambda i: i - block if i // block % 2 else i + block, to_first)
     odd = permute(odd, lambda i: i + block if i // block % 2 else i - block)
     even = permute(
         even, lambda i: i - block if i // block % 2 else i + block, lambda i: not to_first(i)

time: 36.3 us -> 36 us (level)
  no operation moved by 1% of the time
where the time goes in v5:
time: 36 us; the launch traced here: 35.7 us
  starting transfers between devices  23.1 us (64%)
  Pallas kernels  8.83 us (25%)
  waiting for transfers between devices  3.59 us (10%)
    ppermute x5, starting transfers between devices, permute(): return lax.ppermute(value, AXES, pairs)  14.9 us
    all_to_all x1, starting transfers between devices, local(): nodes = lax.all_to_all(chunk, 'near', 0, 0)  8.25 us
    pallas_call x1, Pallas kernels, local(): call(early_kernel, [((4, 32, 256), F32), ((12, 256, 256), BF16), ((128, 1...  3.66 us
    all_to_all x1, waiting for transfers between devices, local(): nodes = lax.all_to_all(chunk, 'near', 0, 0)  3.58 us
    pallas_call x1, Pallas kernels, local(): call(moments_kernel, [((4, 32, 256), BF16), ((4, 64, 256), BF16), ((4, 64...  2.14 us
    pallas_call x1, Pallas kernels, local(): call(product_kernel, [((4, 32, 256), F32)], [VMEM] * 7, [pltpu.VMEM((4, 3...  1.04 us
    pallas_call x1, Pallas kernels, local(): call(near_kernel, [((4, 32, 256), F32), ((128, 1024), BF16)], [VMEM] * 10...  1.01 us
    pallas_call x1, Pallas kernels, local(): call(levels_kernel, [((3, 32, 128), BF16), ((3, 32, 128), BF16), ((3, 32,...  0.98 us
  transfers between devices with their start and end apart: 6, of which 1 were waited for; matrix products, arithmetic and copies ran while one was open for 0% of the time, Pallas kernels for 6%

profile of v5, /device:TPU:1, one launch (start us, length us, event | category | flops | bytes accessed | tf_op | source)
XLA Modules:
  0.0 35.7 jit_solution(7681964526847254140)
XLA Ops:
  0.0 2.1 %shard_map.91 = (bf16[4,32,256]{2,1,0:T(8,128)(2,1)S(1)}, bf16[4,64,256]{2,1,0:T(8,128)(2,1)S(1)}, bf16[4,64,64]{2,1,0:T(8,128)(2,1)S(1)}, bf16[16,32,128]{2,1,0...) custom-call(bf16[4,32,256]{2,1,0:T(8,128)(2,1)} %x_hbm.1, ...), custom_call_target="tpu_custom_call" | custom-call | tf_op jit(solution)/shard_map/pallas_call | solution.py:328
  2.2 3.7 %shard_map.92 = (f32[4,32,256]{2,1,0:T(8,128)S(1)}, bf16[12,256,256]{2,1,0:T(8,128)(2,1)S(1)}, bf16[128,1024]{1,0:T(8,128)(2,1)S(1)}) custom-call(bf16[4,32,256]{2,1,0:T(8,128)(2,1)S(1)} %get-tuple-element.28.x_ref, bf16[4,64,64]{2,1,0:T(8,128)(2,1)S(1)} %get-tuple-element.30.transfer_ref, bf16[4,64,256]{2,1,0:T(8,128)(2,1)S(1)} %get-tuple-element.31.basis_ref, ...), custom_call_target="tpu_custom_call" | custom-call | tf_op jit(solution)/shard_map/pallas_call | solution.py:360
  5.8 8.2 %all-to-all-start = ((bf16[16,32,128]{2,1,0:T(8,128)(2,1)}), bf16[16,32,128]{2,1,0:T(8,128)(2,1)S(1)}, u32[]{:S(2)}, u32[]{:S(2)}) async-start(bf16[16,32,128]{2,1,0:T(8,128)(2,1)} %get-tuple-element.37), calls=%async_computation | async-start | bytes 262144 | tf_op jit(solution)/shard_map/all_to_all | solution.py:374
  14.1 2.0 %collective-permute-start = (bf16[5,32,256]{2,1,0:T(8,128)(2,1)S(1)}, bf16[5,32,256]{2,1,0:T(8,128)(2,1)S(1)}, u32[]{:S(2)}, u32[]{:S(2)}) collective-permute-start(bf16[5,32,256]{2,1,0:T(8,128)(2,1)S(1)} %get-tuple-element.35), channel_id=1, source_target_pairs={{0,1},{1,0},{2,3},{3,2},{4,5},{5,4},{6,7},{7,6},{8,9},{9,8},{10,11... | collective-permute-start | bytes 245768 | tf_op jit(solution)/shard_map/ppermute | solution.py:313
  16.1 3.6 %collective-permute-start.1 = (bf16[5,32,256]{2,1,0:T(8,128)(2,1)S(1)}, bf16[5,32,256]{2,1,0:T(8,128)(2,1)S(1)}, u32[]{:S(2)}, u32[]{:S(2)}) collective-permute-start(bf16[5,32,256]{2,1,0:T(8,128)(2,1)S(1)} %get-tuple-element.36), channel_id=1, source_target_pairs={{0,511},{1,2},{2,1},{3,4},{4,3},{5,6},{6,5},{7,8},{8,7},{9,10},{10... | collective-permute-start | bytes 245768 | tf_op jit(solution)/shard_map/ppermute | solution.py:313
  19.7 3.6 %all-to-all-done.nodes_ref = bf16[16,32,128]{2,1,0:T(8,128)(2,1)S(1)} async-done(((bf16[16,32,128]{2,1,0:T(8,128)(2,1)}), bf16[16,32,128]{2,1,0:T(8,128)(2,1)S(1)}, u32[]{:S(2)}, u32[]{:S(2)}) %all-to-all-start) | async-done | bytes 131104 | tf_op jit(solution)/shard_map/all_to_all | solution.py:374
  23.2 1.0 %shard_map.93 = (bf16[3,32,128]{2,1,0:T(8,128)(2,1)S(1)}, bf16[3,32,128]{2,1,0:T(8,128)(2,1)S(1)}, bf16[3,32,128]{2,1,0:T(8,128)(2,1)S(1)}, f32[32,64]{1,0:T(8,128)S(1)}) custom-call(bf16[16,32,128]{2,1,0:T(8,128)(2,1)S(1)} %all-to-all-done.nodes_ref, bf16[3,2,64,64]{3,2,1,0:T(8,128)(2,1)S(1)} %get-tuple-element.38.level_ref, ...), custom_call_target="tpu_custom_call" | custom-call | tf_op jit(solution)/shard_map/pallas_call | solution.py:377
  24.2 1.3 %collective-permute-start.2 = (bf16[3,32,128]{2,1,0:T(8,128)(2,1)S(1)}, bf16[3,32,128]{2,1,0:T(8,128)(2,1)S(1)}, u32[]{:S(2)}, u32[]{:S(2)}) collective-permute-start(bf16[3,32,128]{2,1,0:T(8,128)(2,1)S(1)} %get-tuple-element.47), channel_id=1, source_target_pairs={{0,16},{17,1},{18,2},{19,3},{20,4},{21,5},{22,6},{23,7},{24,8},{25... | collective-permute-start | bytes 73736 | tf_op jit(solution)/shard_map/ppermute | solution.py:313
  25.5 6.7 %collective-permute-start.3 = (bf16[3,32,128]{2,1,0:T(8,128)(2,1)S(1)}, bf16[3,32,128]{2,1,0:T(8,128)(2,1)S(1)}, u32[]{:S(2)}, u32[]{:S(2)}) collective-permute-start(bf16[3,32,128]{2,1,0:T(8,128)(2,1)S(1)} %get-tuple-element.48), channel_id=1, source_target_pairs={{0,496},{1,497},{2,498},{3,499},{4,500},{5,501},{6,502},{7,503},{8... | collective-permute-start | bytes 73736 | tf_op jit(solution)/shard_map/ppermute | solution.py:313
  32.3 1.3 %collective-permute-start.4 = (bf16[3,32,128]{2,1,0:T(8,128)(2,1)S(1)}, bf16[3,32,128]{2,1,0:T(8,128)(2,1)S(1)}, u32[]{:S(2)}, u32[]{:S(2)}) collective-permute-start(bf16[3,32,128]{2,1,0:T(8,128)(2,1)S(1)} %get-tuple-element.49), channel_id=1, source_target_pairs={{1,17},{2,18},{3,19},{4,20},{5,21},{6,22},{7,23},{8,24},{9,25},{10... | collective-permute-start | bytes 73736 | tf_op jit(solution)/shard_map/ppermute | solution.py:313
  33.6 0.0 collective-permute-done.sibling_ref
  33.6 0.0 collective-permute-done.1.next_ref
  33.6 1.0 %shard_map.94 = (f32[4,32,256]{2,1,0:T(8,128)S(1)}, bf16[128,1024]{1,0:T(8,128)(2,1)S(1)}) custom-call(bf16[4,32,256]{2,1,0:T(8,128)(2,1)S(1)} %get-tuple-element.28.x_ref, bf16[5,32,256]{2,1,0:T(8,128)(2,1)S(1)} %collective-permute-done.sibling_ref, bf16[5,32,256]{2,1,0:T(8,128)(2,1)S(1)} %collective-permute-done.1.next_ref, ...), custom_call_target="tpu_custom_call" | custom-call | flops 200000000 | bytes 4000000 | tf_op jit(solution)/shard_map/pallas_call | solution.py:396
  34.6 0.0 collective-permute-done.2.first_ref
  34.6 0.0 collective-permute-done.3.odd_ref
  34.6 0.0 collective-permute-done.4.even_ref
  34.6 1.0 %shard_map.95 = f32[4,32,256]{2,1,0:T(8,128)} custom-call(f32[4,32,256]{2,1,0:T(8,128)S(1)} %get-tuple-element.46.near_ref, bf16[3,32,128]{2,1,0:T(8,128)(2,1)S(1)} %collective-permute-done.2.first_ref, bf16[3,32,128]{2,1,0:T(8,128)(2,1)S(1)} %collective-permute-done.3.odd_ref, bf16[3,32,128]{2,1,0:T(8,128)(2,1)S(1)} %collective-permute-done.4.even_ref, ...), custom_call_target="tpu_custom_call" | custom-call | tf_op jit(solution)/shard_map/pallas_call | solution.py:421
Async XLA Ops:
  5.8 17.4 %all-to-all-start = ((bf16[16,32,128]{2,1,0:T(8,128)(2,1)}), bf16[16,32,128]{2,1,0:T(8,128)(2,1)S(1)}, u32[]{:S(2)}, u32[]{:S(2)}) async-start(bf16[16,32,128]{2,1,0:T(8,128)(2,1)} %get-tuple-element.37), calls=%async_computation | async-start | bytes 262144 | tf_op jit(solution)/shard_map/all_to_all | solution.py:374
  14.1 19.5 %collective-permute-start = (bf16[5,32,256]{2,1,0:T(8,128)(2,1)S(1)}, bf16[5,32,256]{2,1,0:T(8,128)(2,1)S(1)}, u32[]{:S(2)}, u32[]{:S(2)}) collective-permute-start(bf16[5,32,256]{2,1,0:T(8,128)(2,1)S(1)} %get-tuple-element.35), channel_id=1, source_target_pairs={{0,1},{1,0},{2,3},{3,2},{4,5},{5,4},{6,7},{7,6},{8,9},{9,8},{10,11... | collective-permute-start | bytes 245768 | tf_op jit(solution)/shard_map/ppermute | solution.py:313
  16.1 17.5 %collective-permute-start.1 = (bf16[5,32,256]{2,1,0:T(8,128)(2,1)S(1)}, bf16[5,32,256]{2,1,0:T(8,128)(2,1)S(1)}, u32[]{:S(2)}, u32[]{:S(2)}) collective-permute-start(bf16[5,32,256]{2,1,0:T(8,128)(2,1)S(1)} %get-tuple-element.36), channel_id=1, source_target_pairs={{0,511},{1,2},{2,1},{3,4},{4,3},{5,6},{6,5},{7,8},{8,7},{9,10},{10... | collective-permute-start | bytes 245768 | tf_op jit(solution)/shard_map/ppermute | solution.py:313
  24.2 10.4 %collective-permute-start.2 = (bf16[3,32,128]{2,1,0:T(8,128)(2,1)S(1)}, bf16[3,32,128]{2,1,0:T(8,128)(2,1)S(1)}, u32[]{:S(2)}, u32[]{:S(2)}) collective-permute-start(bf16[3,32,128]{2,1,0:T(8,128)(2,1)S(1)} %get-tuple-element.47), channel_id=1, source_target_pairs={{0,16},{17,1},{18,2},{19,3},{20,4},{21,5},{22,6},{23,7},{24,8},{25... | collective-permute-start | bytes 73736 | tf_op jit(solution)/shard_map/ppermute | solution.py:313
  25.5 9.1 %collective-permute-start.3 = (bf16[3,32,128]{2,1,0:T(8,128)(2,1)S(1)}, bf16[3,32,128]{2,1,0:T(8,128)(2,1)S(1)}, u32[]{:S(2)}, u32[]{:S(2)}) collective-permute-start(bf16[3,32,128]{2,1,0:T(8,128)(2,1)S(1)} %get-tuple-element.48), channel_id=1, source_target_pairs={{0,496},{1,497},{2,498},{3,499},{4,500},{5,501},{6,502},{7,503},{8... | collective-permute-start | bytes 73736 | tf_op jit(solution)/shard_map/ppermute | solution.py:313
  32.3 2.4 %collective-permute-start.4 = (bf16[3,32,128]{2,1,0:T(8,128)(2,1)S(1)}, bf16[3,32,128]{2,1,0:T(8,128)(2,1)S(1)}, u32[]{:S(2)}, u32[]{:S(2)}) collective-permute-start(bf16[3,32,128]{2,1,0:T(8,128)(2,1)S(1)} %get-tuple-element.49), channel_id=1, source_target_pairs={{1,17},{2,18},{3,19},{4,20},{5,21},{6,22},{7,23},{8,24},{9,25},{10... | collective-permute-start | bytes 73736 | tf_op jit(solution)/shard_map/ppermute | solution.py:313

commit v6 on v5

--- a/solution.py
+++ b/solution.py
@@ -51,12 +51,15 @@
     near = lax.axis_index("near")
     odd = near % 2
     copies = load(
-        (x_hbm, basis_hbm, transfer_hbm, level_hbm, coupling_hbm, node_hbm, leaf_hbm),
-        (x_ref, basis_ref, transfer_ref, level_ref, coupling, node_ref, leaf_ref),
-        semaphores,
+        (x_hbm, basis_hbm, transfer_hbm), (x_ref, basis_ref, transfer_ref), semaphores
     )
     copies[0].wait()
     copies[1].wait()
+    copies += load(
+        (level_hbm, coupling_hbm, node_hbm, leaf_hbm),
+        (level_ref, coupling, node_ref, leaf_ref),
+        semaphores.at[pl.ds(3, 4)],
+    )
     parts = [halves(dot_nt(x_ref[j], basis_ref[j])) for j in range(4)]
     copies[2].wait()
     weights = stacked([transfer_ref[j] for j in range(4)], 0)

time: 36 us -> 36.6 us (1.017)
  Pallas kernels: 8.83 us -> 9.42 us
    pallas_call x1, Pallas kernels: 2.14 us -> 2.73 us  [local(): call(moments_kernel, [((4, 32, 256), BF16), ((4, 64, 256), BF16), ((4, 64...]
  transfers between devices with their start and end apart: 6 -> 6, of which waited for: 1 -> 1; matrix products, arithmetic and copies ran while one was open for 0% -> 0% of each run, Pallas kernels for 6% -> 5%
where the time goes in v6:
time: 36.6 us; the launch traced here: 36.3 us
  starting transfers between devices  23.1 us (63%)
  Pallas kernels  9.42 us (26%)
  waiting for transfers between devices  3.59 us (10%)
    ppermute x5, starting transfers between devices, permute(): return lax.ppermute(value, AXES, pairs)  14.9 us
    all_to_all x1, starting transfers between devices, local(): nodes = lax.all_to_all(chunk, 'near', 0, 0)  8.25 us
    pallas_call x1, Pallas kernels, local(): call(early_kernel, [((4, 32, 256), F32), ((12, 256, 256), BF16), ((128, 1...  3.66 us
    all_to_all x1, waiting for transfers between devices, local(): nodes = lax.all_to_all(chunk, 'near', 0, 0)  3.58 us
    pallas_call x1, Pallas kernels, local(): call(moments_kernel, [((4, 32, 256), BF16), ((4, 64, 256), BF16), ((4, 64...  2.73 us
    pallas_call x1, Pallas kernels, local(): call(product_kernel, [((4, 32, 256), F32)], [VMEM] * 7, [pltpu.VMEM((4, 3...  1.04 us
    pallas_call x1, Pallas kernels, local(): call(near_kernel, [((4, 32, 256), F32), ((128, 1024), BF16)], [VMEM] * 10...  1.01 us
    pallas_call x1, Pallas kernels, local(): call(levels_kernel, [((3, 32, 128), BF16), ((3, 32, 128), BF16), ((3, 32,...  0.98 us
  transfers between devices with their start and end apart: 6, of which 1 were waited for; matrix products, arithmetic and copies ran while one was open for 0% of the time, Pallas kernels for 5%

profile of v6, /device:TPU:1, one launch (start us, length us, event | category | flops | bytes accessed | tf_op | source)
XLA Modules:
  0.0 36.3 jit_solution(10281203326542621571)
XLA Ops:
  0.0 2.7 %shard_map.91 = (bf16[4,32,256]{2,1,0:T(8,128)(2,1)S(1)}, bf16[4,64,256]{2,1,0:T(8,128)(2,1)S(1)}, bf16[4,64,64]{2,1,0:T(8,128)(2,1)S(1)}, bf16[16,32,128]{2,1,0...) custom-call(bf16[4,32,256]{2,1,0:T(8,128)(2,1)} %x_hbm.1, ...), custom_call_target="tpu_custom_call" | custom-call | tf_op jit(solution)/shard_map/pallas_call | solution.py:331
  2.7 3.7 %shard_map.92 = (f32[4,32,256]{2,1,0:T(8,128)S(1)}, bf16[12,256,256]{2,1,0:T(8,128)(2,1)S(1)}, bf16[128,1024]{1,0:T(8,128)(2,1)S(1)}) custom-call(bf16[4,32,256]{2,1,0:T(8,128)(2,1)S(1)} %get-tuple-element.28.x_ref, bf16[4,64,64]{2,1,0:T(8,128)(2,1)S(1)} %get-tuple-element.30.transfer_ref, bf16[4,64,256]{2,1,0:T(8,128)(2,1)S(1)} %get-tuple-element.31.basis_ref, ...), custom_call_target="tpu_custom_call" | custom-call | tf_op jit(solution)/shard_map/pallas_call | solution.py:363
  6.4 8.2 %all-to-all-start = ((bf16[16,32,128]{2,1,0:T(8,128)(2,1)}), bf16[16,32,128]{2,1,0:T(8,128)(2,1)S(1)}, u32[]{:S(2)}, u32[]{:S(2)}) async-start(bf16[16,32,128]{2,1,0:T(8,128)(2,1)} %get-tuple-element.37), calls=%async_computation | async-start | bytes 262144 | tf_op jit(solution)/shard_map/all_to_all | solution.py:377
  14.7 2.0 %collective-permute-start = (bf16[5,32,256]{2,1,0:T(8,128)(2,1)S(1)}, bf16[5,32,256]{2,1,0:T(8,128)(2,1)S(1)}, u32[]{:S(2)}, u32[]{:S(2)}) collective-permute-start(bf16[5,32,256]{2,1,0:T(8,128)(2,1)S(1)} %get-tuple-element.35), channel_id=1, source_target_pairs={{0,1},{1,0},{2,3},{3,2},{4,5},{5,4},{6,7},{7,6},{8,9},{9,8},{10,11... | collective-permute-start | bytes 245768 | tf_op jit(solution)/shard_map/ppermute | solution.py:316
  16.7 3.6 %collective-permute-start.1 = (bf16[5,32,256]{2,1,0:T(8,128)(2,1)S(1)}, bf16[5,32,256]{2,1,0:T(8,128)(2,1)S(1)}, u32[]{:S(2)}, u32[]{:S(2)}) collective-permute-start(bf16[5,32,256]{2,1,0:T(8,128)(2,1)S(1)} %get-tuple-element.36), channel_id=1, source_target_pairs={{0,511},{1,2},{2,1},{3,4},{4,3},{5,6},{6,5},{7,8},{8,7},{9,10},{10... | collective-permute-start | bytes 245768 | tf_op jit(solution)/shard_map/ppermute | solution.py:316
  20.3 3.6 %all-to-all-done.nodes_ref = bf16[16,32,128]{2,1,0:T(8,128)(2,1)S(1)} async-done(((bf16[16,32,128]{2,1,0:T(8,128)(2,1)}), bf16[16,32,128]{2,1,0:T(8,128)(2,1)S(1)}, u32[]{:S(2)}, u32[]{:S(2)}) %all-to-all-start) | async-done | bytes 131104 | tf_op jit(solution)/shard_map/all_to_all | solution.py:377
  23.8 1.0 %shard_map.93 = (bf16[3,32,128]{2,1,0:T(8,128)(2,1)S(1)}, bf16[3,32,128]{2,1,0:T(8,128)(2,1)S(1)}, bf16[3,32,128]{2,1,0:T(8,128)(2,1)S(1)}, f32[32,64]{1,0:T(8,128)S(1)}) custom-call(bf16[16,32,128]{2,1,0:T(8,128)(2,1)S(1)} %all-to-all-done.nodes_ref, bf16[3,2,64,64]{3,2,1,0:T(8,128)(2,1)S(1)} %get-tuple-element.38.level_ref, ...), custom_call_target="tpu_custom_call" | custom-call | tf_op jit(solution)/shard_map/pallas_call | solution.py:380
  24.8 1.3 %collective-permute-start.2 = (bf16[3,32,128]{2,1,0:T(8,128)(2,1)S(1)}, bf16[3,32,128]{2,1,0:T(8,128)(2,1)S(1)}, u32[]{:S(2)}, u32[]{:S(2)}) collective-permute-start(bf16[3,32,128]{2,1,0:T(8,128)(2,1)S(1)} %get-tuple-element.47), channel_id=1, source_target_pairs={{0,16},{17,1},{18,2},{19,3},{20,4},{21,5},{22,6},{23,7},{24,8},{25... | collective-permute-start | bytes 73736 | tf_op jit(solution)/shard_map/ppermute | solution.py:316
  26.1 6.7 %collective-permute-start.3 = (bf16[3,32,128]{2,1,0:T(8,128)(2,1)S(1)}, bf16[3,32,128]{2,1,0:T(8,128)(2,1)S(1)}, u32[]{:S(2)}, u32[]{:S(2)}) collective-permute-start(bf16[3,32,128]{2,1,0:T(8,128)(2,1)S(1)} %get-tuple-element.48), channel_id=1, source_target_pairs={{0,496},{1,497},{2,498},{3,499},{4,500},{5,501},{6,502},{7,503},{8... | collective-permute-start | bytes 73736 | tf_op jit(solution)/shard_map/ppermute | solution.py:316
  32.9 1.3 %collective-permute-start.4 = (bf16[3,32,128]{2,1,0:T(8,128)(2,1)S(1)}, bf16[3,32,128]{2,1,0:T(8,128)(2,1)S(1)}, u32[]{:S(2)}, u32[]{:S(2)}) collective-permute-start(bf16[3,32,128]{2,1,0:T(8,128)(2,1)S(1)} %get-tuple-element.49), channel_id=1, source_target_pairs={{1,17},{2,18},{3,19},{4,20},{5,21},{6,22},{7,23},{8,24},{9,25},{10... | collective-permute-start | bytes 73736 | tf_op jit(solution)/shard_map/ppermute | solution.py:316
  34.2 0.0 collective-permute-done.sibling_ref
  34.2 0.0 collective-permute-done.1.next_ref
  34.2 1.0 %shard_map.94 = (f32[4,32,256]{2,1,0:T(8,128)S(1)}, bf16[128,1024]{1,0:T(8,128)(2,1)S(1)}) custom-call(bf16[4,32,256]{2,1,0:T(8,128)(2,1)S(1)} %get-tuple-element.28.x_ref, bf16[5,32,256]{2,1,0:T(8,128)(2,1)S(1)} %collective-permute-done.sibling_ref, bf16[5,32,256]{2,1,0:T(8,128)(2,1)S(1)} %collective-permute-done.1.next_ref, ...), custom_call_target="tpu_custom_call" | custom-call | flops 200000000 | bytes 4000000 | tf_op jit(solution)/shard_map/pallas_call | solution.py:399
  35.2 0.0 collective-permute-done.2.first_ref
  35.2 0.0 collective-permute-done.3.odd_ref
  35.2 0.0 collective-permute-done.4.even_ref
  35.2 1.0 %shard_map.95 = f32[4,32,256]{2,1,0:T(8,128)} custom-call(f32[4,32,256]{2,1,0:T(8,128)S(1)} %get-tuple-element.46.near_ref, bf16[3,32,128]{2,1,0:T(8,128)(2,1)S(1)} %collective-permute-done.2.first_ref, bf16[3,32,128]{2,1,0:T(8,128)(2,1)S(1)} %collective-permute-done.3.odd_ref, bf16[3,32,128]{2,1,0:T(8,128)(2,1)S(1)} %collective-permute-done.4.even_ref, ...), custom_call_target="tpu_custom_call" | custom-call | tf_op jit(solution)/shard_map/pallas_call | solution.py:424
Async XLA Ops:
  6.4 17.4 %all-to-all-start = ((bf16[16,32,128]{2,1,0:T(8,128)(2,1)}), bf16[16,32,128]{2,1,0:T(8,128)(2,1)S(1)}, u32[]{:S(2)}, u32[]{:S(2)}) async-start(bf16[16,32,128]{2,1,0:T(8,128)(2,1)} %get-tuple-element.37), calls=%async_computation | async-start | bytes 262144 | tf_op jit(solution)/shard_map/all_to_all | solution.py:377
  14.7 19.5 %collective-permute-start = (bf16[5,32,256]{2,1,0:T(8,128)(2,1)S(1)}, bf16[5,32,256]{2,1,0:T(8,128)(2,1)S(1)}, u32[]{:S(2)}, u32[]{:S(2)}) collective-permute-start(bf16[5,32,256]{2,1,0:T(8,128)(2,1)S(1)} %get-tuple-element.35), channel_id=1, source_target_pairs={{0,1},{1,0},{2,3},{3,2},{4,5},{5,4},{6,7},{7,6},{8,9},{9,8},{10,11... | collective-permute-start | bytes 245768 | tf_op jit(solution)/shard_map/ppermute | solution.py:316
  16.7 17.5 %collective-permute-start.1 = (bf16[5,32,256]{2,1,0:T(8,128)(2,1)S(1)}, bf16[5,32,256]{2,1,0:T(8,128)(2,1)S(1)}, u32[]{:S(2)}, u32[]{:S(2)}) collective-permute-start(bf16[5,32,256]{2,1,0:T(8,128)(2,1)S(1)} %get-tuple-element.36), channel_id=1, source_target_pairs={{0,511},{1,2},{2,1},{3,4},{4,3},{5,6},{6,5},{7,8},{8,7},{9,10},{10... | collective-permute-start | bytes 245768 | tf_op jit(solution)/shard_map/ppermute | solution.py:316
  24.8 10.4 %collective-permute-start.2 = (bf16[3,32,128]{2,1,0:T(8,128)(2,1)S(1)}, bf16[3,32,128]{2,1,0:T(8,128)(2,1)S(1)}, u32[]{:S(2)}, u32[]{:S(2)}) collective-permute-start(bf16[3,32,128]{2,1,0:T(8,128)(2,1)S(1)} %get-tuple-element.47), channel_id=1, source_target_pairs={{0,16},{17,1},{18,2},{19,3},{20,4},{21,5},{22,6},{23,7},{24,8},{25... | collective-permute-start | bytes 73736 | tf_op jit(solution)/shard_map/ppermute | solution.py:316
  26.1 9.1 %collective-permute-start.3 = (bf16[3,32,128]{2,1,0:T(8,128)(2,1)S(1)}, bf16[3,32,128]{2,1,0:T(8,128)(2,1)S(1)}, u32[]{:S(2)}, u32[]{:S(2)}) collective-permute-start(bf16[3,32,128]{2,1,0:T(8,128)(2,1)S(1)} %get-tuple-element.48), channel_id=1, source_target_pairs={{0,496},{1,497},{2,498},{3,499},{4,500},{5,501},{6,502},{7,503},{8... | collective-permute-start | bytes 73736 | tf_op jit(solution)/shard_map/ppermute | solution.py:316
  32.9 2.4 %collective-permute-start.4 = (bf16[3,32,128]{2,1,0:T(8,128)(2,1)S(1)}, bf16[3,32,128]{2,1,0:T(8,128)(2,1)S(1)}, u32[]{:S(2)}, u32[]{:S(2)}) collective-permute-start(bf16[3,32,128]{2,1,0:T(8,128)(2,1)S(1)} %get-tuple-element.49), channel_id=1, source_target_pairs={{1,17},{2,18},{3,19},{4,20},{5,21},{6,22},{7,23},{8,24},{9,25},{10... | collective-permute-start | bytes 73736 | tf_op jit(solution)/shard_map/ppermute | solution.py:316
